TPU v7x, 512 devices: a whole 4x4x16 slice. The times are simulated.
512 devices in a mesh: ctx: 32 (over z, x_lo), ch: 16 (over x_hi, y, core).
Axes of the slice: x: 4 (x_hi: 2, x_lo: 2; x = x_hi * 2 + x_lo), y: 4, z: 16, core: 2. Of those that a mesh axis runs over, the one named last changes fastest.
Arguments:
- inputs: bfloat16 [256, 131072], P('ch', 'ctx'), may hold values from -6 to 6
- cotangent: bfloat16 [256, 131072], P('ch', 'ctx'), may hold values from -6 to 6
- filters: float32 [16, 131072], P(None, 'ctx'), may hold values from -6 to 6
Outputs:
- input_grad: bfloat16 [256, 131072], P('ch', 'ctx')
- filter_grad: float32 [16, 131072], P('ch', 'ctx')
All inputs are finite; a program needn't handle non-finite values.
Results may differ from a plain program's by a relative error of at most 0.012.
Values may be sent and summed in bfloat16 or wider, within the bound.
A program may use at most 64 MiB of HBM per device.

v0:
```python
import math

import jax
import jax.numpy as jnp
from jax import lax
from jax.sharding import PartitionSpec as P

HIGHEST = lax.Precision.HIGHEST


def angle_table(left_index, right_index, modulus):
    product = left_index[:, None] * right_index[None, :] % modulus
    angles = product.astype(jnp.float32) * (2.0 * math.pi / modulus)
    return (jnp.cos(angles), jnp.sin(angles))


def integers(number):
    return jnp.arange(number, dtype=jnp.int32)


def matrix_turn(real_part, imag_part, cosine_table, sine_table, formula, direction):
    first_term = jnp.einsum(formula, real_part, cosine_table, precision=HIGHEST)
    second_term = jnp.einsum(formula, imag_part, sine_table, precision=HIGHEST)
    third_term = jnp.einsum(formula, imag_part, cosine_table, precision=HIGHEST)
    fourth_term = jnp.einsum(formula, real_part, sine_table, precision=HIGHEST)
    return (first_term - direction * second_term, third_term + direction * fourth_term)


def point_turn(real_part, imag_part, cosine_table, sine_table, direction):
    new_real = real_part * cosine_table - direction * imag_part * sine_table
    new_imag = imag_part * cosine_table + direction * real_part * sine_table
    return (new_real, new_imag)


def outer_forward(signal, offset):
    blocks = signal.shape[1]
    length = 2 * blocks
    narrow = signal.shape[2]
    full_length = length * blocks * narrow
    cosine_table, sine_table = angle_table(integers(blocks), integers(length), length)
    real_part = jnp.einsum("rdw,dk->rkw", signal, cosine_table, precision=HIGHEST)
    imag_part = -jnp.einsum("rdw,dk->rkw", signal, sine_table, precision=HIGHEST)
    positions = offset + integers(narrow)
    cosine_table, sine_table = angle_table(integers(length), positions, full_length)
    return point_turn(real_part, imag_part, cosine_table, sine_table, -1.0)


def inner_forward(real_part, imag_part):
    row_count, pair_count, length = real_part.shape
    lane_count = 128
    rounds = length // lane_count
    real_part = real_part.reshape(row_count, pair_count, rounds, lane_count)
    imag_part = imag_part.reshape(row_count, pair_count, rounds, lane_count)
    cosine_table, sine_table = angle_table(integers(rounds), integers(rounds), rounds)
    real_part, imag_part = matrix_turn(
        real_part, imag_part, cosine_table, sine_table, "rxab,ak->rxkb", -1.0
    )
    cosine_table, sine_table = angle_table(integers(rounds), integers(lane_count), length)
    real_part, imag_part = point_turn(real_part, imag_part, cosine_table, sine_table, -1.0)
    cosine_table, sine_table = angle_table(integers(lane_count), integers(lane_count), lane_count)
    return matrix_turn(real_part, imag_part, cosine_table, sine_table, "rxkb,bl->rxkl", -1.0)


def inner_inverse(real_part, imag_part):
    row_count, pair_count, rounds, lane_count = real_part.shape
    length = rounds * lane_count
    cosine_table, sine_table = angle_table(integers(lane_count), integers(lane_count), lane_count)
    real_part, imag_part = matrix_turn(
        real_part, imag_part, cosine_table, sine_table, "rxkl,lb->rxkb", 1.0
    )
    cosine_table, sine_table = angle_table(integers(rounds), integers(lane_count), length)
    real_part, imag_part = point_turn(real_part, imag_part, cosine_table, sine_table, 1.0)
    cosine_table, sine_table = angle_table(integers(rounds), integers(rounds), rounds)
    real_part, imag_part = matrix_turn(
        real_part, imag_part, cosine_table, sine_table, "rxkb,ka->rxab", 1.0
    )
    return (
        real_part.reshape(row_count, pair_count, length),
        imag_part.reshape(row_count, pair_count, length),
    )


def outer_inverse(real_part, imag_part, offset):
    length = real_part.shape[1]
    blocks = length // 2
    narrow = real_part.shape[2]
    full_length = length * blocks * narrow
    positions = offset + integers(narrow)
    cosine_table, sine_table = angle_table(integers(length), positions, full_length)
    real_part, imag_part = point_turn(real_part, imag_part, cosine_table, sine_table, 1.0)
    cosine_table, sine_table = angle_table(integers(length), integers(blocks), length)
    result = jnp.einsum("rkw,kd->rdw", real_part, cosine_table, precision=HIGHEST)
    result = result - jnp.einsum("rkw,kd->rdw", imag_part, sine_table, precision=HIGHEST)
    return result * (1.0 / full_length)


def shards(inputs, cotangent, filters):
    context_count = lax.axis_size("ctx")
    channel_count, length = inputs.shape
    filter_count = filters.shape[0]
    narrow = length // context_count
    offset = lax.axis_index("ctx") * narrow
    factor = (length * context_count) ** (-0.5)

    def rows_back(pieces):
        return outer_inverse(pieces[0], pieces[1], offset)

    pieces = (
        lax.all_to_all(
            inputs.reshape(channel_count, 1, length), "ctx", split_axis=2, concat_axis=1, tiled=True
        ),
        lax.all_to_all(
            cotangent.reshape(channel_count, 1, length),
            "ctx",
            split_axis=2,
            concat_axis=1,
            tiled=True,
        ),
    )
    signal_real, signal_imag = outer_forward(pieces[0].astype(jnp.float32), offset)
    upstream_real, upstream_imag = outer_forward(pieces[1].astype(jnp.float32), offset)
    part_a = signal_real
    part_b = signal_imag
    part_c = upstream_real
    part_d = upstream_imag
    pieces = (
        lax.all_to_all(part_a, "ctx", split_axis=1, concat_axis=2, tiled=True),
        lax.all_to_all(part_b, "ctx", split_axis=1, concat_axis=2, tiled=True),
        lax.all_to_all(part_c, "ctx", split_axis=1, concat_axis=2, tiled=True),
        lax.all_to_all(part_d, "ctx", split_axis=1, concat_axis=2, tiled=True),
    )
    signal_real, signal_imag = inner_forward(pieces[0], pieces[1])
    upstream_real, upstream_imag = inner_forward(pieces[2], pieces[3])
    signal_real, signal_imag, upstream_real, upstream_imag = (
        signal_real,
        signal_imag,
        upstream_real,
        upstream_imag,
    )
    filter_real, filter_imag = outer_forward(
        lax.all_to_all(
            filters.reshape(-1, 1, length), "ctx", split_axis=2, concat_axis=1, tiled=True
        ),
        offset,
    )
    pieces = (
        lax.all_to_all(filter_real, "ctx", split_axis=1, concat_axis=2, tiled=True),
        lax.all_to_all(filter_imag, "ctx", split_axis=1, concat_axis=2, tiled=True),
    )
    kernel_real, kernel_imag = inner_forward(pieces[0], pieces[1])
    grouped = (channel_count // filter_count, filter_count) + signal_real.shape[1:]
    signal_real = signal_real.reshape(grouped)
    signal_imag = signal_imag.reshape(grouped)
    upstream_real = upstream_real.reshape(grouped)
    upstream_imag = upstream_imag.reshape(grouped)
    input_real = (kernel_real * upstream_real + kernel_imag * upstream_imag).reshape(
        (channel_count,) + grouped[2:]
    )
    input_imag = (kernel_real * upstream_imag - kernel_imag * upstream_real).reshape(
        (channel_count,) + grouped[2:]
    )
    cross_real = jnp.sum(signal_real * upstream_real + signal_imag * upstream_imag, axis=0)
    cross_imag = jnp.sum(signal_real * upstream_imag - signal_imag * upstream_real, axis=0)
    wave_real, wave_imag = inner_inverse(input_real, input_imag)
    returned = rows_back(
        (
            lax.all_to_all(wave_real, "ctx", split_axis=2, concat_axis=1, tiled=True),
            lax.all_to_all(wave_imag, "ctx", split_axis=2, concat_axis=1, tiled=True),
        )
    )
    returned = lax.all_to_all(
        returned.astype(jnp.bfloat16), "ctx", split_axis=1, concat_axis=2, tiled=True
    ).astype(returned.dtype)
    input_grad = (returned.reshape(channel_count, length) * factor).astype(jnp.bfloat16)
    wave_real, wave_imag = inner_inverse(cross_real, cross_imag)
    filter_back = rows_back(
        (
            lax.all_to_all(
                wave_real.astype(jnp.bfloat16), "ctx", split_axis=2, concat_axis=1, tiled=True
            ).astype(wave_real.dtype),
            lax.all_to_all(
                wave_imag.astype(jnp.bfloat16), "ctx", split_axis=2, concat_axis=1, tiled=True
            ).astype(wave_imag.dtype),
        )
    )
    filter_back = lax.all_to_all(filter_back, "ctx", split_axis=1, concat_axis=2, tiled=True)
    filter_grad = filter_back.reshape(-1, length)
    filter_grad = lax.psum_scatter(filter_grad, "ch", scatter_dimension=0, tiled=True)
    return (input_grad, filter_grad * factor)


def solution(mesh):
    return jax.shard_map(
        shards,
        mesh=mesh,
        in_specs=(P("ch", "ctx"), P("ch", "ctx"), P(None, "ctx")),
        out_specs=(P("ch", "ctx"), P("ch", "ctx")),
        check_vma=False,
    )
```

profile of v0, /device:TPU:6, one launch (start us, length us, event | category | flops | bytes accessed | tf_op | source)
XLA Modules:
  0.0 730.3 jit_solution(13700812604735130213)
XLA Ops:
  7.2 4.3 copy.85
  12.0 22.4 %reduce = bf16[4096,16]{1,0:T(8,128)(2,1)S(1)} reduce(bf16[4096,1,16]{2,1,0:T(2,128)(2,1)S(1)} %bitcast.294, bf16[]{:T(256)} %broadcast.666), dimensions={1}, to_apply=%bitcast.256.reduce_sub_computation | reduce | bytes 262146
  36.2 17.0 %all-to-all-start.9 = ((bf16[32,2,1024]{2,1,0:T(2,128)(2,1)}), bf16[32,2,1024]{2,1,0:T(2,128)(2,1)S(1)}, u32[]{:S(2)}, u32[]{:S(2)}) async-start(bf16[32,2,1024]{2,1,0:T(2,128)(2,1)} %reshape.215), calls=%async_computation.9 | async-start | bytes 262144 | tf_op jit(solution)/shard_map/all_to_all | solution.py:109
  56.0 22.4 %reduce.3 = bf16[4096,16]{1,0:T(8,128)(2,1)S(1)} reduce(bf16[4096,1,16]{2,1,0:T(2,128)(2,1)S(1)} %bitcast.296, bf16[]{:T(256)} %broadcast.666), dimensions={1}, to_apply=%bitcast.250.reduce_sub_computation | reduce | bytes 262146
  80.2 13.4 %all-to-all-start.3 = ((bf16[32,2,1024]{2,1,0:T(2,128)(2,1)}), bf16[32,2,1024]{2,1,0:T(2,128)(2,1)S(1)}, u32[]{:S(2)}, u32[]{:S(2)}) async-start(bf16[32,2,1024]{2,1,0:T(2,128)(2,1)} %reshape.209), calls=%async_computation.3 | async-start | bytes 262144 | tf_op jit(solution)/shard_map/all_to_all | solution.py:112
  95.8 19.4 %reduce.1 = f32[4096,16]{1,0:T(8,128)} reduce(f32[4096,1,16]{2,1,0:T(1,128)S(1)} %bitcast.295, f32[]{:T(128)} %broadcast.667), dimensions={1}, to_apply=%bitcast.248.reduce_sub_computation | reduce | bytes 524292
  115.1 3.0 reshape.207
  118.1 13.8 %all-to-all-start = ((f32[32,1,2048]{2,1,0:T(1,128)}), f32[32,1,2048]{2,1,0:T(1,128)}, u32[]{:S(2)}, u32[]{:S(2)}) async-start(f32[32,1,2048]{2,1,0:T(1,128)} %reshape.207), calls=%async_computation | async-start | bytes 524288 | tf_op jit(solution)/shard_map/all_to_all | solution.py:141
  142.1 10.1 %all-to-all-done = f32[32,1,2048]{2,1,0:T(1,128)} async-done(((f32[32,1,2048]{2,1,0:T(1,128)}), f32[32,1,2048]{2,1,0:T(1,128)}, u32[]{:S(2)}, u32[]{:S(2)}) %all-to-all-start) | async-done | bytes 262176 | tf_op jit(solution)/shard_map/all_to_all | solution.py:141
  154.4 3.9 reshape.208
  164.3 4.1 all-to-all-start.5
  169.5 30.1 %all-to-all-done.5 = f32[16,64,128]{2,0,1:T(8,128)S(1)} async-done(((f32[16,64,128]{2,0,1:T(8,128)}), f32[16,64,128]{2,0,1:T(8,128)S(1)}, u32[]{:S(2)}, u32[]{:S(2)}) %all-to-all-start.5) | async-done | bytes 524320 | tf_op jit(solution)/shard_map/all_to_all | solution.py:130
  199.6 4.1 all-to-all-start.4
  204.9 29.9 %all-to-all-done.4 = f32[16,64,128]{2,0,1:T(8,128)S(1)} async-done(((f32[16,64,128]{2,0,1:T(8,128)}), f32[16,64,128]{2,0,1:T(8,128)S(1)}, u32[]{:S(2)}, u32[]{:S(2)}) %all-to-all-start.4) | async-done | bytes 524320 | tf_op jit(solution)/shard_map/all_to_all | solution.py:129
  234.8 4.1 all-to-all-start.11
  240.0 30.0 %all-to-all-done.11 = f32[16,64,128]{2,0,1:T(8,128)S(1)} async-done(((f32[16,64,128]{2,0,1:T(8,128)}), f32[16,64,128]{2,0,1:T(8,128)S(1)}, u32[]{:S(2)}, u32[]{:S(2)}) %all-to-all-start.11) | async-done | bytes 524320 | tf_op jit(solution)/shard_map/all_to_all | solution.py:128
  270.0 4.1 all-to-all-start.1
  275.2 30.0 %all-to-all-done.1 = f32[16,64,128]{2,0,1:T(8,128)S(1)} async-done(((f32[16,64,128]{2,0,1:T(8,128)}), f32[16,64,128]{2,0,1:T(8,128)S(1)}, u32[]{:S(2)}, u32[]{:S(2)}) %all-to-all-start.1) | async-done | bytes 524320 | tf_op jit(solution)/shard_map/all_to_all | solution.py:147
  305.2 4.4 all-to-all-start.2
  317.9 22.7 %all-to-all-done.2 = f32[16,64,128]{2,0,1:T(8,128)S(1)} async-done(((f32[16,64,128]{2,0,1:T(8,128)}), f32[16,64,128]{2,0,1:T(8,128)S(1)}, u32[]{:S(2)}, u32[]{:S(2)}) %all-to-all-start.2) | async-done | bytes 524320 | tf_op jit(solution)/shard_map/all_to_all | solution.py:148
  340.6 4.8 all-to-all-start.10
  357.6 18.3 %all-to-all-done.10 = f32[16,64,128]{2,0,1:T(8,128)} async-done(((f32[16,64,128]{2,0,1:T(8,128)}), f32[16,64,128]{2,0,1:T(8,128)}, u32[]{:S(2)}, u32[]{:S(2)}) %all-to-all-start.10) | async-done | bytes 524320 | tf_op jit(solution)/shard_map/all_to_all | solution.py:127
  394.3 3.1 copy.105
  400.3 5.1 all-to-all-start.13
  412.6 11.7 %all-to-all-done.13 = bf16[32,2,2048]{2,1,0:T(2,128)(2,1)} async-done(((bf16[32,2,2048]{2,1,0:T(2,128)(2,1)}), bf16[32,2,2048]{2,1,0:T(2,128)(2,1)}, u32[]{:S(2)}, u32[]{:S(2)}) %all-to-all-start.13) | async-done | bytes 262176 | tf_op jit(solution)/shard_map/all_to_all | solution.py:181
  424.3 4.7 all-to-all-start.12
  432.0 3.1 copy.103
  435.1 8.0 %reshape.211 = f32[32,1,4096]{2,1,0:T(1,128)} reshape(f32[4096,2,16]{2,1,0:T(2,128)} %bitcast.285) | data formatting | bytes 1048576
  443.1 4.1 all-to-all-done.12
  447.2 9.4 %all-to-all-start.7 = ((f32[32,1,4096]{2,1,0:T(1,128)}), f32[32,1,4096]{2,1,0:T(1,128)S(1)}, u32[]{:S(2)}, u32[]{:S(2)}) async-start(f32[32,1,4096]{2,1,0:T(1,128)} %reshape.211), calls=%async_computation.7 | async-start | bytes 1048576 | tf_op jit(solution)/shard_map/all_to_all | solution.py:168
  457.9 3.1 copy.102
  461.0 7.9 %reshape.213 = f32[32,1,4096]{2,1,0:T(1,128)} reshape(f32[4096,2,16]{2,1,0:T(2,128)} %bitcast.286) | data formatting | bytes 1048576
  468.9 16.1 %all-to-all-done.7 = f32[32,1,4096]{2,1,0:T(1,128)S(1)} async-done(((f32[32,1,4096]{2,1,0:T(1,128)}), f32[32,1,4096]{2,1,0:T(1,128)S(1)}, u32[]{:S(2)}, u32[]{:S(2)}) %all-to-all-start.7) | async-done | bytes 524320 | tf_op jit(solution)/shard_map/all_to_all | solution.py:168
  485.0 4.8 all-to-all-start.6
  489.8 7.1 reshape.218
  496.9 3.7 convert_bitcast_fusion
  500.6 5.2 copy.94
  505.8 7.1 reshape.220
  513.0 3.7 convert_bitcast_fusion.1
  516.6 5.2 copy.92
  523.8 13.2 %all-to-all-start.14 = ((f32[16,32,128]{2,0,1:T(8,128)}), f32[16,32,128]{2,0,1:T(8,128)S(1)}, u32[]{:S(2)}, u32[]{:S(2)}) async-start(f32[16,32,128]{2,0,1:T(8,128)} %copy.95), calls=%async_computation.14 | async-start | bytes 524288 | tf_op jit(solution)/shard_map/all_to_all | solution.py:186
  538.9 7.2 reshape.212
  546.1 5.2 copy.82
  551.3 2.9 reduce.5
  554.3 6.9 reshape.214
  561.2 5.2 copy.80
  568.9 13.1 %all-to-all-start.8 = ((bf16[16,32,128]{2,0,1:T(8,128)(2,1)}), bf16[16,32,128]{2,0,1:T(8,128)(2,1)S(1)}, u32[]{:S(2)}, u32[]{:S(2)}) async-start(bf16[16,32,128]{2,0,1:T(8,128)(2,1)} %copy.83), calls=%async_computation.8 | async-start | bytes 262144 | tf_op jit(solution)/shard_map/all_to_all | solution.py:171
  583.2 137.0 %all-reduce.3.cloned.1.call-done = f32[16,4096]{1,0:T(8,128)} async-done(((f32[16,4096]{1,0:T(8,128)}), f32[16,4096]{1,0:T(8,128)}) %all-reduce.3.cloned.1.call-update) | async-done | bytes 262160
  (118 shorter events, 94.8 us)
Async XLA Ops:
  12.0 41.3 %copy-start.12 = (bf16[16,4096]{1,0:T(8,128)(2,1)S(1)}, bf16[16,4096]{1,0:T(8,128)(2,1)}, u32[]{:S(2)}) copy-start(bf16[16,4096]{1,0:T(8,128)(2,1)} %param.4) | copy-start | bytes 393220
  36.2 44.0 %all-to-all-start.9 = ((bf16[32,2,1024]{2,1,0:T(2,128)(2,1)}), bf16[32,2,1024]{2,1,0:T(2,128)(2,1)S(1)}, u32[]{:S(2)}, u32[]{:S(2)}) async-start(bf16[32,2,1024]{2,1,0:T(2,128)(2,1)} %reshape.215), calls=%async_computation.9 | async-start | bytes 262144 | tf_op jit(solution)/shard_map/all_to_all | solution.py:109
  80.2 37.9 %all-to-all-start.3 = ((bf16[32,2,1024]{2,1,0:T(2,128)(2,1)}), bf16[32,2,1024]{2,1,0:T(2,128)(2,1)S(1)}, u32[]{:S(2)}, u32[]{:S(2)}) async-start(bf16[32,2,1024]{2,1,0:T(2,128)(2,1)} %reshape.209), calls=%async_computation.3 | async-start | bytes 262144 | tf_op jit(solution)/shard_map/all_to_all | solution.py:112
  118.1 34.1 %all-to-all-start = ((f32[32,1,2048]{2,1,0:T(1,128)}), f32[32,1,2048]{2,1,0:T(1,128)}, u32[]{:S(2)}, u32[]{:S(2)}) async-start(f32[32,1,2048]{2,1,0:T(1,128)} %reshape.207), calls=%async_computation | async-start | bytes 524288 | tf_op jit(solution)/shard_map/all_to_all | solution.py:141
  135.9 4.9 copy-start.11
  163.2 5.2 copy-start.6
  163.2 40.6 %copy-start.5 = (f32[16,64,128]{2,1,0:T(8,128)S(1)}, f32[16,64,128]{2,1,0:T(8,128)}, u32[]{:S(2)}) copy-start(f32[16,64,128]{2,1,0:T(8,128)} %get-tuple-element.6) | copy-start | bytes 1572868
  164.3 35.3 %all-to-all-start.5 = ((f32[16,64,128]{2,0,1:T(8,128)}), f32[16,64,128]{2,0,1:T(8,128)S(1)}, u32[]{:S(2)}, u32[]{:S(2)}) async-start(f32[16,64,128]{2,0,1:T(8,128)} %copy.77), calls=%async_computation.5 | async-start | bytes 1048576 | tf_op jit(solution)/shard_map/all_to_all | solution.py:130
  199.6 35.2 %all-to-all-start.4 = ((f32[16,64,128]{2,0,1:T(8,128)}), f32[16,64,128]{2,0,1:T(8,128)S(1)}, u32[]{:S(2)}, u32[]{:S(2)}) async-start(f32[16,64,128]{2,0,1:T(8,128)} %copy.75), calls=%async_computation.4 | async-start | bytes 1048576 | tf_op jit(solution)/shard_map/all_to_all | solution.py:129
  234.8 35.2 %all-to-all-start.11 = ((f32[16,64,128]{2,0,1:T(8,128)}), f32[16,64,128]{2,0,1:T(8,128)S(1)}, u32[]{:S(2)}, u32[]{:S(2)}) async-start(f32[16,64,128]{2,0,1:T(8,128)} %copy.89), calls=%async_computation.11 | async-start | bytes 1048576 | tf_op jit(solution)/shard_map/all_to_all | solution.py:128
  270.0 35.2 %all-to-all-start.1 = ((f32[16,64,128]{2,0,1:T(8,128)}), f32[16,64,128]{2,0,1:T(8,128)S(1)}, u32[]{:S(2)}, u32[]{:S(2)}) async-start(f32[16,64,128]{2,0,1:T(8,128)} %copy.69), calls=%async_computation.1 | async-start | bytes 1048576 | tf_op jit(solution)/shard_map/all_to_all | solution.py:147
  305.2 10.1 %copy-start.2 = (f32[16,64,128]{2,0,1:T(8,128)}, f32[16,64,128]{2,0,1:T(8,128)S(1)}, u32[]{:S(2)}) copy-start(f32[16,64,128]{2,0,1:T(8,128)S(1)} %all-to-all-done.1) | copy-start | bytes 1572868
  305.2 35.4 %all-to-all-start.2 = ((f32[16,64,128]{2,0,1:T(8,128)}), f32[16,64,128]{2,0,1:T(8,128)S(1)}, u32[]{:S(2)}, u32[]{:S(2)}) async-start(f32[16,64,128]{2,0,1:T(8,128)} %copy.71), calls=%async_computation.2 | async-start | bytes 1048576 | tf_op jit(solution)/shard_map/all_to_all | solution.py:148
  340.6 35.3 %all-to-all-start.10 = ((f32[16,64,128]{2,0,1:T(8,128)}), f32[16,64,128]{2,0,1:T(8,128)}, u32[]{:S(2)}, u32[]{:S(2)}) async-start(f32[16,64,128]{2,0,1:T(8,128)} %copy.87), calls=%async_computation.10 | async-start | bytes 1048576 | tf_op jit(solution)/shard_map/all_to_all | solution.py:127
  345.4 4.8 copy-start.3
  354.3 23.5 %copy-start.4 = (f32[32,16,2,128]{3,0,2,1:T(8,128)S(1)}, f32[32,16,2,128]{3,0,2,1:T(8,128)}, u32[]{:S(2)}) copy-start(f32[32,16,2,128]{3,0,2,1:T(8,128)} %fusion.29) | copy-start | bytes 1572868
  379.8 2.6 copy-start.10
  382.4 2.1 copy-start.9
  383.7 1.7 copy-start.8
  384.5 1.7 copy-start.7
  400.3 24.0 %all-to-all-start.13 = ((bf16[32,2,2048]{2,1,0:T(2,128)(2,1)}), bf16[32,2,2048]{2,1,0:T(2,128)(2,1)}, u32[]{:S(2)}, u32[]{:S(2)}) async-start(bf16[32,2,2048]{2,1,0:T(2,128)(2,1)} %reshape.217), calls=%async_computation.13 | async-start | bytes 524288 | tf_op jit(solution)/shard_map/all_to_all | solution.py:181
  406.8 4.2 copy-start
  408.1 3.7 copy-start.1
  424.3 22.9 %all-to-all-start.12 = ((bf16[32,2,2048]{2,1,0:T(2,128)(2,1)}), bf16[32,2,2048]{2,1,0:T(2,128)(2,1)}, u32[]{:S(2)}, u32[]{:S(2)}) async-start(bf16[32,2,2048]{2,1,0:T(2,128)(2,1)} %reshape.219), calls=%async_computation.12 | async-start | bytes 524288 | tf_op jit(solution)/shard_map/all_to_all | solution.py:178
  447.2 37.9 %all-to-all-start.7 = ((f32[32,1,4096]{2,1,0:T(1,128)}), f32[32,1,4096]{2,1,0:T(1,128)S(1)}, u32[]{:S(2)}, u32[]{:S(2)}) async-start(f32[32,1,4096]{2,1,0:T(1,128)} %reshape.211), calls=%async_computation.7 | async-start | bytes 1048576 | tf_op jit(solution)/shard_map/all_to_all | solution.py:168
  485.0 38.8 %all-to-all-start.6 = ((f32[32,1,4096]{2,1,0:T(1,128)}), f32[32,1,4096]{2,1,0:T(1,128)}, u32[]{:S(2)}, u32[]{:S(2)}) async-start(f32[32,1,4096]{2,1,0:T(1,128)} %reshape.213), calls=%async_computation.6 | async-start | bytes 1048576 | tf_op jit(solution)/shard_map/all_to_all | solution.py:167
  523.8 42.7 %all-to-all-start.14 = ((f32[16,32,128]{2,0,1:T(8,128)}), f32[16,32,128]{2,0,1:T(8,128)S(1)}, u32[]{:S(2)}, u32[]{:S(2)}) async-start(f32[16,32,128]{2,0,1:T(8,128)} %copy.95), calls=%async_computation.14 | async-start | bytes 524288 | tf_op jit(solution)/shard_map/all_to_all | solution.py:186
  537.0 183.3 %all-reduce.3.cloned.1.call-start = ((), (), s32[]{:S(2)}) async-start(), calls=%async_computation.15 | async-start | bytes 524288
  568.9 153.4 %all-to-all-start.8 = ((bf16[16,32,128]{2,0,1:T(8,128)(2,1)}), bf16[16,32,128]{2,0,1:T(8,128)(2,1)S(1)}, u32[]{:S(2)}, u32[]{:S(2)}) async-start(bf16[16,32,128]{2,0,1:T(8,128)(2,1)} %copy.83), calls=%async_computation.8 | async-start | bytes 262144 | tf_op jit(solution)/shard_map/all_to_all | solution.py:171
Sparse Core Ops, SparseCore 0:
  567.3 152.9 all-reduce.2
where the time goes:
time: 740 us; the launch traced here: 730 us
  waiting for transfers between devices  340 us (46%)
  local copies, waits for them, and re-layouts  120 us (16%)
  starting transfers between devices  120 us (16%)
  other arithmetic  81.8 us (11%)
  matrix products  53 us (7%)
  between operations  15.3 us (2%)
    unnamed x2, waiting for transfers between devices  137 us
    unnamed x46, local copies, waits for them, and re-layouts  68 us
    unnamed x3, other arithmetic  64.2 us
    all_to_all x1, waiting for transfers between devices, shards(): lax.all_to_all(part_d, 'ctx', split_axis=1, concat_axis=2, tiled=True)  30.1 us
    all_to_all x1, waiting for transfers between devices, shards(): lax.all_to_all(filter_real, 'ctx', split_axis=1, concat_axis=2, tiled=True)  30 us
    all_to_all x1, waiting for transfers between devices, shards(): lax.all_to_all(part_b, 'ctx', split_axis=1, concat_axis=2, tiled=True)  30 us
    all_to_all x1, waiting for transfers between devices, shards(): lax.all_to_all(part_c, 'ctx', split_axis=1, concat_axis=2, tiled=True)  29.9 us
    all_to_all x1, waiting for transfers between devices, shards(): lax.all_to_all(filter_imag, 'ctx', split_axis=1, concat_axis=2, tiled=True)  22.7 us
  transfers between devices with their start and end apart: 16, of which 11 were waited for; matrix products, arithmetic and copies ran while one was open for 26% of the time, Pallas kernels for 0%

commit v1 on v0

v1 whole, which is shorter than its diff:
```python
import functools
import math

import jax
import jax.numpy as jnp
import ml_dtypes
import numpy as np
from jax import lax
from jax.experimental import pallas as pl
from jax.experimental.pallas import tpu as pltpu
from jax.sharding import PartitionSpec as P

ROWS = 16
BF16 = jnp.bfloat16
F32 = jnp.float32


def split_halves(table):
    high = table.astype(ml_dtypes.bfloat16)
    low = (table - high.astype(np.float64)).astype(ml_dtypes.bfloat16)
    return high, low


def make_tables(outer, inner, tile):
    length = outer * inner
    k1 = np.arange(outer) + 0.25
    n1 = np.arange(outer)
    n2 = np.arange(inner)
    angle = 2 * np.pi * ((4 * np.outer(np.arange(outer), n1) + n1[None, :]) % (4 * outer)) / (4 * outer)
    cosine, sine = np.cos(angle), np.sin(angle)
    steps = outer // tile
    cosine_high, cosine_low = split_halves(cosine)
    sine_high, sine_low = split_halves(-sine)
    forward = np.concatenate(
        [part.reshape(steps, tile, outer) for part in (cosine_high, sine_high, cosine_low, sine_low)], axis=1
    )
    back_high, back_low = split_halves(np.concatenate([cosine.T, sine.T], axis=1) * (length ** -1.5))
    backward = np.concatenate(
        [part.reshape(steps, tile, 2 * outer) for part in (back_high, back_low)], axis=1
    )
    angle = 2 * np.pi * np.outer(k1, n2) / length
    twiddle = np.concatenate([np.cos(angle), -np.sin(angle)], axis=1).astype(np.float32)
    angle = 2 * np.pi * (np.outer(n2, n2) % inner) / inner
    wave_real, wave_imag = np.cos(angle), -np.sin(angle)
    wave = np.block([[wave_real, wave_imag], [-wave_imag, wave_real]])
    wave_high, wave_low = split_halves(wave)
    return forward, np.concatenate([wave_high, wave_low], axis=0), twiddle, backward


def dot(left, right):
    return jnp.dot(left, right, preferred_element_type=F32)


def halves(value):
    high = value.astype(BF16)
    return high, (value - high.astype(F32)).astype(BF16)


def kernel(
    sizes, tile,
    inputs_ref, cotangent_ref, filters_ref, forward_hbm, wave_hbm, twiddle_hbm, backward_hbm,
    input_grad_ref, filter_grad_ref,
    staged, staged_filter, first, second, spectrum, parts, result_narrow, result_wide, arrived, reduced_in,
    reduced_out, grad_in, forward_ref, wave_ref, twiddle_ref, backward_ref,
    table_sem, send_sem, filter_send_sem, gather_send_sem, pass_send_sem, out_send_sem, reduce_send_sem,
    last_send_sem, first_sem, part_sem, gather_sem, pass_sem, out_sem, reduce_sem, last_sem,
):
    zs, groups, outer, inner = sizes
    blocks = 2 * zs
    ctx = lax.axis_index("ctx")
    ch = lax.axis_index("ch")
    z, xl = ctx // 2, ctx % 2
    plane, core = ch // 2, ch % 2
    place = 2 * plane + xl
    is_self = lambda c, g: jnp.logical_and(c == ctx, g == ch)

    tables = [
        pltpu.make_async_copy(forward_hbm, forward_ref, table_sem.at[0]),
        pltpu.make_async_copy(wave_hbm, wave_ref, table_sem.at[1]),
        pltpu.make_async_copy(twiddle_hbm, twiddle_ref, table_sem.at[2]),
        pltpu.make_async_copy(backward_hbm, backward_ref, table_sem.at[3]),
    ]
    for table in tables:
        table.start()

    def remote(src, dst, ssem, rsem, to_ctx, to_ch):
        return pltpu.make_async_remote_copy(
            src_ref=src, dst_ref=dst, send_sem=ssem, recv_sem=rsem,
            device_id={"ctx": to_ctx, "ch": to_ch}, device_id_type=pl.DeviceIdType.MESH,
        )

    def start(src, dst, ssem, rsem, to_ctx, to_ch):
        own = is_self(to_ctx, to_ch)

        @pl.when(own)
        def _():
            pltpu.make_async_copy(src, dst, rsem).start()

        @pl.when(jnp.logical_not(own))
        def _():
            remote(src, dst, ssem, rsem, to_ctx, to_ch).start()

    def finish(src, dst, ssem, rsem, to_ctx, to_ch):
        @pl.when(jnp.logical_not(is_self(to_ctx, to_ch)))
        def _():
            remote(src, dst, ssem, rsem, to_ctx, to_ch).wait_send()

    def landed(ref, sem):
        pltpu.make_async_copy(ref, ref, sem).wait()

    barrier = pltpu.get_barrier_semaphore()

    def greet(to_ctx, to_ch):
        @pl.when(jnp.logical_not(is_self(to_ctx, to_ch)))
        def _():
            pl.semaphore_signal(
                barrier, inc=1, device_id={"ctx": to_ctx, "ch": to_ch}, device_id_type=pl.DeviceIdType.MESH
            )

    def greet_sources(j, carry):
        greet(j, 2 * plane + xl)
        return carry

    def greet_plane(q, carry):
        greet(2 * z + q % 2, 2 * (q // 2) + core)
        return carry

    lax.fori_loop(0, blocks, greet_sources, 0)
    lax.fori_loop(0, groups, greet_plane, 0)
    last_from_ctx = 2 * ch + z % 2
    last_from_ch = 2 * (z // 2) + 1
    greet(last_from_ctx, last_from_ch)

    count = zs * ROWS
    row = lax.broadcasted_iota(jnp.int32, (count, count), 0)
    col = lax.broadcasted_iota(jnp.int32, (count, count), 1)
    regroup = jnp.logical_and(row // ROWS == col % zs, row % ROWS == col // zs).astype(F32).astype(BF16)
    ungroup = jnp.logical_and(row % zs == col // ROWS, row // zs == col % ROWS).astype(F32).astype(BF16)

    def stage(value):
        stacked = jnp.concatenate([value[:, a * inner:(a + 1) * inner] for a in range(ROWS)], axis=0)
        return dot(regroup, stacked.astype(BF16)).astype(BF16).reshape(zs, ROWS, inner)

    staged[0] = stage(cotangent_ref[...].astype(F32))
    staged[1] = stage(inputs_ref[...].astype(F32))

    @pl.when(ch == z)
    def _():
        staged_filter[...] = stage(filters_ref[...])

    own_chip = (xl == core).astype(jnp.int32)
    expected = 2 * zs - own_chip + groups - 1
    own_last_0 = is_self(2 * place, z).astype(jnp.int32)
    own_last_1 = is_self(2 * place + 1, z).astype(jnp.int32)
    expected = expected + core * (2 - own_last_0 - own_last_1)
    pl.semaphore_wait(barrier, expected)

    def order(i):
        k = zs - 1 - i
        step = (k + 1) // 2
        off = jnp.where(k % 2 == 1, step, zs - step)
        return (z + off) % zs

    def rows(c):
        def args(i):
            f = order(i)
            return staged.at[c, f], first.at[ctx], send_sem.at[c, i], first_sem, 2 * f + core, 2 * plane + c
        return args

    def filter_rows(i):
        f = order(i)
        return staged_filter.at[f], second.at[ctx], filter_send_sem.at[i], part_sem, 2 * f + core, 2 * plane

    def both(function, *many):
        def body(i, carry):
            for args in many:
                function(*args(i))
            return carry
        return body

    @pl.when(ch == z)
    def _():
        lax.fori_loop(0, zs, both(start, filter_rows), 0)

    lax.fori_loop(0, zs, both(start, rows(0), rows(1)), 0)

    def gather(q):
        def args():
            block = second.at[pl.ds(2 * place, 2)]
            return block, block, gather_send_sem.at[q], gather_sem, 2 * z + q % 2, 2 * (q // 2)
        return args

    def gather_each(function):
        def body(k, carry):
            q = (place + 1 + k) % groups
            function(*gather(q)())
            return carry
        return body

    @pl.when(core == 0)
    def _():
        landed(second.at[pl.ds(2 * place, 2)], part_sem)
        lax.fori_loop(0, groups - 1, gather_each(start), 0)

    def transform(source, k):
        rows_at = pl.ds(pl.multiple_of(k * tile, tile), tile)
        flat = source[...].reshape(outer, inner)
        both_parts = dot(forward_ref[k], flat)
        real = both_parts[:tile] + both_parts[2 * tile:3 * tile]
        imag = both_parts[tile:2 * tile] + both_parts[3 * tile:]
        return turn(real, imag, rows_at)

    def turn(real, imag, rows_at):
        cosine = twiddle_ref[rows_at, :inner]
        sine = twiddle_ref[rows_at, inner:]
        return real * cosine - imag * sine, real * sine + imag * cosine

    def inner_transform(real, imag):
        high, low = halves(jnp.concatenate([real, imag], axis=1))
        wave_high = wave_ref[:2 * inner]
        total = dot(jnp.concatenate([high, low], axis=0), wave_high)
        return total[:tile] + total[tile:] + dot(high, wave_ref[2 * inner:])

    landed(first, first_sem)

    to_partner = (first, second, pass_send_sem, pass_sem, ctx, 2 * plane + 1)

    @pl.when(core == 0)
    def _():
        remote(*to_partner).start()

    for table in tables[:3]:
        table.wait()

    def first_pass(k, carry):
        rows_at = pl.ds(pl.multiple_of(k * tile, tile), tile)
        spectrum[rows_at, :] = inner_transform(*transform(first, k))
        return carry

    steps = outer // tile
    lax.fori_loop(0, steps, first_pass, 0)

    @pl.when(core == 0)
    def _():
        landed(second.at[pl.ds(0, blocks - 2)], gather_sem)

    @pl.when(core == 1)
    def _():
        landed(second, pass_sem)

    sign = (1 - 2 * core).astype(F32)

    def second_pass(k, carry):
        rows_at = pl.ds(pl.multiple_of(k * tile, tile), tile)
        other = inner_transform(*transform(second, k))
        mine = spectrum[rows_at, :]
        real_a, imag_a = mine[:, :inner], mine[:, inner:]
        real_b, imag_b = other[:, :inner], other[:, inner:]
        real = real_a * real_b + imag_a * imag_b
        imag = (real_a * imag_b - imag_a * real_b) * sign
        back = inner_transform(real, imag)
        real, imag = turn(back[:, :inner], back[:, inner:], rows_at)
        lower_at = pl.ds(pl.multiple_of(outer + k * tile, tile), tile)
        parts[0, rows_at, :], parts[1, rows_at, :] = halves(real)
        parts[0, lower_at, :], parts[1, lower_at, :] = halves(imag)
        return carry

    lax.fori_loop(0, steps, second_pass, 0)
    tables[3].wait()

    per_tile = tile // ROWS

    def last_pass(k, carry):
        table = backward_ref[k]
        total = dot(table, parts[0])
        total = total[:tile] + total[tile:] + dot(table[:tile], parts[1])
        total = total.reshape(per_tile, ROWS, inner)
        at = pl.ds(k * per_tile, per_tile)

        @pl.when(core == 0)
        def _():
            result_narrow[at] = total.astype(BF16)

        @pl.when(core == 1)
        def _():
            result_wide[at] = total

        return carry

    lax.fori_loop(0, steps, last_pass, 0)

    def out_rows(x):
        def args(i):
            j = 2 * order(i) + x
            return result_narrow.at[j], arrived.at[z], out_send_sem.at[j], out_sem, j, 2 * plane + xl
        return args

    def reduce_rows(k):
        q = (place + k) % groups
        return (
            result_wide.at[pl.ds(2 * q, 2)], reduced_in.at[place], reduce_send_sem.at[q], reduce_sem,
            2 * z + q % 2, 2 * (q // 2) + 1,
        )

    def last_rows(i):
        return reduced_out.at[i], grad_in, last_send_sem.at[i], last_sem, 2 * place + i, z

    @pl.when(core == 0)
    def _():
        lax.fori_loop(0, zs, both(start, out_rows(0), out_rows(1)), 0)

    @pl.when(core == 1)
    def _():
        lax.fori_loop(0, groups, both(start, reduce_rows), 0)
        landed(reduced_in, reduce_sem)
        total = reduced_in[0]
        for q in range(1, groups):
            total = total + reduced_in[q]
        reduced_out[...] = total
        lax.fori_loop(0, 2, both(start, last_rows), 0)

    landed(arrived, out_sem)
    spread = dot(ungroup, arrived[...].reshape(count, inner)).astype(BF16)
    for a in range(ROWS):
        input_grad_ref[:, a * inner:(a + 1) * inner] = spread[a * zs:(a + 1) * zs]
    landed(grad_in, last_sem)
    for a in range(ROWS):
        filter_grad_ref[:, a * inner:(a + 1) * inner] = grad_in[a:a + 1]

    lax.fori_loop(0, zs, both(finish, rows(0), rows(1)), 0)

    @pl.when(ch == z)
    def _():
        lax.fori_loop(0, zs, both(finish, filter_rows), 0)

    @pl.when(core == 0)
    def _():
        lax.fori_loop(0, groups - 1, gather_each(finish), 0)
        remote(*to_partner).wait_send()
        lax.fori_loop(0, zs, both(finish, out_rows(0), out_rows(1)), 0)

    @pl.when(core == 1)
    def _():
        lax.fori_loop(0, groups, both(finish, reduce_rows), 0)
        lax.fori_loop(0, 2, both(finish, last_rows), 0)


def shards(tables, inputs, cotangent, filters):
    zs = lax.axis_size("ctx") // 2
    groups = lax.axis_size("ch")
    rows, length = inputs.shape
    inner = length // ROWS
    blocks = 2 * zs
    outer = blocks * ROWS
    tile = min(outer, 256)
    assert rows == zs and groups == zs and filters.shape[0] == zs
    vmem = pl.BlockSpec(memory_space=pltpu.VMEM)
    hbm = pl.BlockSpec(memory_space=pl.ANY)
    dma = pltpu.SemaphoreType.DMA
    return pl.pallas_call(
        functools.partial(kernel, (zs, groups, outer, inner), tile),
        out_shape=(
            jax.ShapeDtypeStruct((rows, length), BF16),
            jax.ShapeDtypeStruct((1, length), F32),
        ),
        in_specs=[vmem] * 3 + [hbm] * 4,
        out_specs=(vmem, vmem),
        scratch_shapes=[
            pltpu.VMEM((2, zs, ROWS, inner), BF16),
            pltpu.VMEM((zs, ROWS, inner), BF16),
            pltpu.VMEM((blocks, ROWS, inner), BF16),
            pltpu.VMEM((blocks, ROWS, inner), BF16),
            pltpu.VMEM((outer, 2 * inner), F32),
            pltpu.VMEM((2, 2 * outer, inner), BF16),
            pltpu.VMEM((blocks, ROWS, inner), BF16),
            pltpu.VMEM((blocks, ROWS, inner), F32),
            pltpu.VMEM((zs, ROWS, inner), BF16),
            pltpu.VMEM((groups, 2, ROWS, inner), F32),
            pltpu.VMEM((2, ROWS, inner), F32),
            pltpu.VMEM((ROWS, inner), F32),
            *[pltpu.VMEM(table.shape, table.dtype) for table in tables],
            dma((4,)), dma((2, zs)), dma((zs,)), dma((groups,)), dma, dma((blocks,)), dma((groups,)),
            dma((2,)), dma, dma, dma, dma, dma, dma, dma,
        ],
        compiler_params=pltpu.CompilerParams(
            collective_id=0, has_side_effects=True, vmem_limit_bytes=48 * 1024 * 1024
        ),
    )(inputs, cotangent, filters, *tables)


def solution(mesh):
    blocks = mesh.shape["ctx"]
    inner = 256
    outer = blocks * ROWS
    tables = make_tables(outer, inner, min(outer, 256))

    def whole(inputs, cotangent, filters):
        body = functools.partial(shards, tuple(jnp.asarray(table) for table in tables))
        return jax.shard_map(
            body,
            mesh=mesh,
            in_specs=(P("ch", "ctx"), P("ch", "ctx"), P(None, "ctx")),
            out_specs=(P("ch", "ctx"), P("ch", "ctx")),
            check_vma=False,
        )(inputs, cotangent, filters)

    return whole
```

time: 740 us -> 64.5 us (0.09); the launches traced: 730 us -> 64.2 us
  waiting for transfers between devices: 340 us -> 0 us
  starting transfers between devices: 120 us -> 0 us
  local copies, waits for them, and re-layouts: 120 us -> 8.05 us
  other arithmetic: 81.8 us -> 0 us
  Pallas kernels: 0 us -> 55.5 us
  matrix products: 53 us -> 0 us
  between operations: 15.3 us -> 0.65 us
    all_to_all x15 -> x0, waiting for transfers between devices: 203 us -> none  [the longest x1 30.1 us: shards(): lax.all_to_all(part_d, 'ctx', split_axis=1, concat_axis=2, tiled=True)]
    unnamed x2 -> x0, waiting for transfers between devices: 137 us -> none
    all_to_all x15 -> x0, starting transfers between devices: 120 us -> none  [the longest x1 17 us: shards(): lax.all_to_all(inputs.reshape(channel_count, 1, length), 'ctx', split_axi...]
    unnamed x3 -> x0, other arithmetic: 64.2 us -> none
    unnamed x46 -> x14, local copies, waits for them, and re-layouts: 68 us -> 8.05 us
    pallas_call x0 -> x1, Pallas kernels: none -> 55.5 us  [shards(): pl.pallas_call(functools.partial(kernel, (zs, groups, outer, inner), tile...]
    dot_general x50 -> x0, matrix products: 53 us -> none  [the longest x10 12.3 us: matrix_turn(): first_term = jnp.einsum(formula, real_part, cosine_table, precision=HIGHEST)]
    convert_element_type x5 -> x0, local copies, waits for them, and re-layouts: 15.5 us -> none  [the longest x2 10.5 us: shards(): filter_back = rows_back((lax.all_to_all(wave_real.astype(jnp.bfloat16), '...]
  transfers between devices with their start and end apart: 16 -> 0, of which waited for: 11 -> 0; matrix products, arithmetic and copies ran while one was open for 26% -> 0% of each run, Pallas kernels for 0% -> 0%
where the time goes in v1:
time: 64.5 us; the launch traced here: 64.2 us
  Pallas kernels  55.5 us (86%)
  local copies, waits for them, and re-layouts  8.05 us (12%)
  between operations  0.65 us (1%)
    pallas_call x1, Pallas kernels, shards(): pl.pallas_call(functools.partial(kernel, (zs, groups, outer, inner), tile...  55.5 us
    unnamed x14, local copies, waits for them, and re-layouts  8.05 us

profile of v1, /device:TPU:6, one launch (start us, length us, event | category | flops | bytes accessed | tf_op | source)
XLA Modules:
  0.0 64.2 jit_solution(1104965219776839257)
XLA Ops:
  0.6 0.0 copy-start
  0.6 1.6 %copy-done = bf16[2,1024,512]{2,1,0:T(8,128)(2,1)S(1)} copy-done((bf16[2,1024,512]{2,1,0:T(8,128)(2,1)S(1)}, bf16[2,1024,512]{2,1,0:T(8,128)(2,1)}, u32[]{:S(2)}) %copy-start) | copy-done | bytes 2097176
  2.2 0.0 copy-start.1
  2.2 1.2 %copy-done.1 = f32[512,512]{1,0:T(8,128)S(1)} copy-done((f32[512,512]{1,0:T(8,128)S(1)}, f32[512,512]{1,0:T(8,128)}, u32[]{:S(2)}) %copy-start.1) | copy-done | bytes 1048600
  3.5 0.0 copy-start.2
  3.5 1.2 %copy-done.2 = bf16[1024,512]{1,0:T(8,128)(2,1)S(1)} copy-done((bf16[1024,512]{1,0:T(8,128)(2,1)S(1)}, bf16[1024,512]{1,0:T(8,128)(2,1)}, u32[]{:S(2)}) %copy-start.2) | copy-done | bytes 1048600
  4.7 0.0 copy-start.3
  4.7 0.9 %copy-done.3 = f32[16,4096]{1,0:T(8,128)S(1)} copy-done((f32[16,4096]{1,0:T(8,128)S(1)}, f32[16,4096]{1,0:T(8,128)}, u32[]{:S(2)}) %copy-start.3) | copy-done | bytes 262168
  5.6 0.0 copy-start.4
  5.6 0.9 %copy-done.4 = bf16[16,4096]{1,0:T(8,128)(2,1)S(1)} copy-done((bf16[16,4096]{1,0:T(8,128)(2,1)S(1)}, bf16[16,4096]{1,0:T(8,128)(2,1)}, u32[]{:S(2)}) %copy-start.4) | copy-done | bytes 131096
  6.5 0.0 copy-start.5
  6.5 0.9 %copy-done.5 = bf16[16,4096]{1,0:T(8,128)(2,1)S(1)} copy-done((bf16[16,4096]{1,0:T(8,128)(2,1)S(1)}, bf16[16,4096]{1,0:T(8,128)(2,1)}, u32[]{:S(2)}) %copy-start.5) | copy-done | bytes 131096
  7.4 55.5 %shard_map.86 = (bf16[16,4096]{1,0:T(8,128)(2,1)S(1)}, f32[1,4096]{1,0:T(1,128)S(1)}) custom-call(bf16[16,4096]{1,0:T(8,128)(2,1)S(1)} %copy-done.4, bf16[16,4096]{1,0:T(8,128)(2,1)S(1)} %copy-done.5, f32[16,4096]{1,0:T(8,128)S(1)} %copy-done.3, bf16[2,1024,512]{2,1,0:T(8,128)(2,1)S(1)} %copy-done, bf16[1024,512]{1,0:T(8,128)(2,1)S(1)} %copy-done.2, ...), custom_call_target="tpu_custom_call" | custom-call | tf_op jit(solution)/shard_map/pallas_call | solution.py:360
  63.0 0.7 %copy.11 = bf16[16,4096]{1,0:T(8,128)(2,1)} copy(bf16[16,4096]{1,0:T(8,128)(2,1)S(1)} %get-tuple-element.4) | data formatting | bytes 262144
  63.6 0.6 copy.12
Async XLA Ops:
  0.6 1.6 %copy-start = (bf16[2,1024,512]{2,1,0:T(8,128)(2,1)S(1)}, bf16[2,1024,512]{2,1,0:T(8,128)(2,1)}, u32[]{:S(2)}) copy-start(bf16[2,1024,512]{2,1,0:T(8,128)(2,1)} %constant.8.clone.forward_hbm) | copy-start | bytes 6291460
  2.2 1.2 %copy-start.1 = (f32[512,512]{1,0:T(8,128)S(1)}, f32[512,512]{1,0:T(8,128)}, u32[]{:S(2)}) copy-start(f32[512,512]{1,0:T(8,128)} %constant.10.clone.twiddle_hbm) | copy-start | bytes 3145732
  3.5 1.2 %copy-start.2 = (bf16[1024,512]{1,0:T(8,128)(2,1)S(1)}, bf16[1024,512]{1,0:T(8,128)(2,1)}, u32[]{:S(2)}) copy-start(bf16[1024,512]{1,0:T(8,128)(2,1)} %constant.9.clone.wave_hbm) | copy-start | bytes 3145732
  4.7 0.9 %copy-start.3 = (f32[16,4096]{1,0:T(8,128)S(1)}, f32[16,4096]{1,0:T(8,128)}, u32[]{:S(2)}) copy-start(f32[16,4096]{1,0:T(8,128)} %filters_ref.1) | copy-start | bytes 786436
  5.6 0.9 %copy-start.4 = (bf16[16,4096]{1,0:T(8,128)(2,1)S(1)}, bf16[16,4096]{1,0:T(8,128)(2,1)}, u32[]{:S(2)}) copy-start(bf16[16,4096]{1,0:T(8,128)(2,1)} %inputs_ref.1) | copy-start | bytes 393220
  6.5 0.9 %copy-start.5 = (bf16[16,4096]{1,0:T(8,128)(2,1)S(1)}, bf16[16,4096]{1,0:T(8,128)(2,1)}, u32[]{:S(2)}) copy-start(bf16[16,4096]{1,0:T(8,128)(2,1)} %cotangent_ref.1) | copy-start | bytes 393220

commit v2 on v1

--- a/solution.py
+++ b/solution.py
@@ -58,11 +58,11 @@
 
 def kernel(
     sizes, tile,
-    inputs_ref, cotangent_ref, filters_ref, forward_hbm, wave_hbm, twiddle_hbm, backward_hbm,
+    inputs_hbm, cotangent_hbm, filters_hbm, forward_hbm, wave_hbm, twiddle_hbm, backward_hbm,
     input_grad_ref, filter_grad_ref,
-    staged, staged_filter, first, second, spectrum, parts, result_narrow, result_wide, arrived, reduced_in,
+    inputs_ref, cotangent_ref, filters_ref, staged, staged_filter, first, second, spectrum, parts, result_narrow, result_wide, arrived, reduced_in,
     reduced_out, grad_in, forward_ref, wave_ref, twiddle_ref, backward_ref,
-    table_sem, send_sem, filter_send_sem, gather_send_sem, pass_send_sem, out_send_sem, reduce_send_sem,
+    load_sem, table_sem, send_sem, filter_send_sem, gather_send_sem, pass_send_sem, out_send_sem, reduce_send_sem,
     last_send_sem, first_sem, part_sem, gather_sem, pass_sem, out_sem, reduce_sem, last_sem,
 ):
     zs, groups, outer, inner = sizes
@@ -80,8 +80,13 @@
         pltpu.make_async_copy(twiddle_hbm, twiddle_ref, table_sem.at[2]),
         pltpu.make_async_copy(backward_hbm, backward_ref, table_sem.at[3]),
     ]
-    for table in tables:
-        table.start()
+    loads = [
+        pltpu.make_async_copy(cotangent_hbm, cotangent_ref, load_sem.at[0]),
+        pltpu.make_async_copy(inputs_hbm, inputs_ref, load_sem.at[1]),
+        pltpu.make_async_copy(filters_hbm, filters_ref, load_sem.at[2]),
+    ]
+    for copy in loads + tables:
+        copy.start()
 
     def remote(src, dst, ssem, rsem, to_ctx, to_ch):
         return pltpu.make_async_remote_copy(
@@ -141,8 +146,11 @@
         stacked = jnp.concatenate([value[:, a * inner:(a + 1) * inner] for a in range(ROWS)], axis=0)
         return dot(regroup, stacked.astype(BF16)).astype(BF16).reshape(zs, ROWS, inner)
 
+    loads[0].wait()
     staged[0] = stage(cotangent_ref[...].astype(F32))
+    loads[1].wait()
     staged[1] = stage(inputs_ref[...].astype(F32))
+    loads[2].wait()
 
     @pl.when(ch == z)
     def _():
@@ -352,10 +360,10 @@
     inner = length // ROWS
     blocks = 2 * zs
     outer = blocks * ROWS
-    tile = min(outer, 256)
+    tile = min(outer, 512)
     assert rows == zs and groups == zs and filters.shape[0] == zs
     vmem = pl.BlockSpec(memory_space=pltpu.VMEM)
-    hbm = pl.BlockSpec(memory_space=pl.ANY)
+    hbm = pl.BlockSpec(memory_space=pltpu.HBM)
     dma = pltpu.SemaphoreType.DMA
     return pl.pallas_call(
         functools.partial(kernel, (zs, groups, outer, inner), tile),
@@ -363,9 +371,12 @@
             jax.ShapeDtypeStruct((rows, length), BF16),
             jax.ShapeDtypeStruct((1, length), F32),
         ),
-        in_specs=[vmem] * 3 + [hbm] * 4,
+        in_specs=[hbm] * 7,
         out_specs=(vmem, vmem),
         scratch_shapes=[
+            pltpu.VMEM((rows, length), BF16),
+            pltpu.VMEM((rows, length), BF16),
+            pltpu.VMEM((rows, length), F32),
             pltpu.VMEM((2, zs, ROWS, inner), BF16),
             pltpu.VMEM((zs, ROWS, inner), BF16),
             pltpu.VMEM((blocks, ROWS, inner), BF16),
@@ -379,11 +390,11 @@
             pltpu.VMEM((2, ROWS, inner), F32),
             pltpu.VMEM((ROWS, inner), F32),
             *[pltpu.VMEM(table.shape, table.dtype) for table in tables],
-            dma((4,)), dma((2, zs)), dma((zs,)), dma((groups,)), dma, dma((blocks,)), dma((groups,)),
+            dma((3,)), dma((4,)), dma((2, zs)), dma((zs,)), dma((groups,)), dma, dma((blocks,)), dma((groups,)),
             dma((2,)), dma, dma, dma, dma, dma, dma, dma,
         ],
         compiler_params=pltpu.CompilerParams(
-            collective_id=0, has_side_effects=True, vmem_limit_bytes=48 * 1024 * 1024
+            collective_id=0, has_side_effects=True, vmem_limit_bytes=64 * 1024 * 1024
         ),
     )(inputs, cotangent, filters, *tables)
 
@@ -392,7 +403,7 @@
     blocks = mesh.shape["ctx"]
     inner = 256
     outer = blocks * ROWS
-    tables = make_tables(outer, inner, min(outer, 256))
+    tables = make_tables(outer, inner, min(outer, 512))
 
     def whole(inputs, cotangent, filters):
         body = functools.partial(shards, tuple(jnp.asarray(table) for table in tables))

time: 64.5 us -> 58.3 us (0.904)
  local copies, waits for them, and re-layouts: 8.05 us -> 2.89 us
  Pallas kernels: 55.5 us -> 54.6 us
    unnamed x14 -> x2, local copies, waits for them, and re-layouts: 8.05 us -> 2.89 us
    pallas_call x1, Pallas kernels: 55.5 us -> 54.6 us  [shards(): pl.pallas_call(functools.partial(kernel, (zs, groups, outer, inner), tile...]
where the time goes in v2:
time: 58.3 us; the launch traced here: 58.1 us
  Pallas kernels  54.6 us (94%)
  local copies, waits for them, and re-layouts  2.89 us (5%)
  between operations  0.64 us (1%)
    pallas_call x1, Pallas kernels, shards(): pl.pallas_call(functools.partial(kernel, (zs, groups, outer, inner), tile...  54.6 us
    unnamed x2, local copies, waits for them, and re-layouts  2.89 us

profile of v2, /device:TPU:6, one launch (start us, length us, event | category | flops | bytes accessed | tf_op | source)
XLA Modules:
  0.0 58.1 jit_solution(4293187845551862509)
XLA Ops:
  0.6 54.6 %shard_map.86 = (bf16[16,4096]{1,0:T(8,128)(2,1)}, f32[1,4096]{1,0:T(1,128)}) custom-call(bf16[16,4096]{1,0:T(8,128)(2,1)} %inputs_hbm.1, bf16[16,4096]{1,0:T(8,128)(2,1)} %cotangent_hbm.1, f32[16,4096]{1,0:T(8,128)} %filters_hbm.1, bf16[1,2048,512]{2,1,0:T(8,128)(2,1)} %constant.8.clone.forward_hbm, bf16[1024,512]{1,0:T(8,128)(2,1)} %constant.9.clone.wave_hbm, ...), custom_call_target="tpu_custom_call" | custom-call | tf_op jit(solution)/shard_map/pallas_call | solution.py:368
  55.2 1.6 %copy.11 = bf16[16,4096]{1,0:T(8,128)(2,1)} copy(bf16[16,4096]{1,0:T(8,128)(2,1)} %get-tuple-element.4) | data formatting | bytes 262144
  56.8 1.3 %copy.12 = f32[1,4096]{1,0:T(1,128)} copy(f32[1,4096]{1,0:T(1,128)} %get-tuple-element.5) | data formatting | bytes 32768

commit v3 on v2

v3 whole, which is shorter than its diff:
```python
import functools
import math

import jax
import jax.numpy as jnp
import ml_dtypes
import numpy as np
from jax import lax
from jax.experimental import pallas as pl
from jax.experimental.pallas import tpu as pltpu
from jax.sharding import PartitionSpec as P

ROWS = 16
BF16 = jnp.bfloat16
F32 = jnp.float32


def split_halves(table):
    high = table.astype(ml_dtypes.bfloat16)
    low = (table - high.astype(np.float64)).astype(ml_dtypes.bfloat16)
    return high, low


def make_tables(outer, inner, tile):
    length = outer * inner
    k1 = np.arange(outer) + 0.25
    n1 = np.arange(outer)
    n2 = np.arange(inner)
    angle = 2 * np.pi * ((4 * np.outer(np.arange(outer), n1) + n1[None, :]) % (4 * outer)) / (4 * outer)
    cosine, sine = np.cos(angle), np.sin(angle)
    steps = outer // tile
    cosine_high, cosine_low = split_halves(cosine)
    sine_high, sine_low = split_halves(-sine)
    forward = np.concatenate(
        [part.reshape(steps, tile, outer) for part in (cosine_high, sine_high, cosine_low, sine_low)], axis=1
    )
    back_high, back_low = split_halves(np.concatenate([cosine.T, sine.T], axis=1) * (length ** -1.5))
    backward = np.concatenate(
        [part.reshape(steps, tile, 2 * outer) for part in (back_high, back_low)], axis=1
    )
    angle = 2 * np.pi * np.outer(k1, n2) / length
    twiddle = np.concatenate([np.cos(angle), -np.sin(angle)], axis=1).astype(np.float32)
    angle = 2 * np.pi * (np.outer(n2, n2) % inner) / inner
    wave_real, wave_imag = np.cos(angle), -np.sin(angle)
    wave = np.block([[wave_real, wave_imag], [-wave_imag, wave_real]])
    wave_high, wave_low = split_halves(wave)
    return forward, np.concatenate([wave_high, wave_low], axis=0), twiddle, backward


def dot(left, right):
    return jnp.dot(left, right, preferred_element_type=F32)


def halves(value):
    high = value.astype(BF16)
    return high, (value - high.astype(F32)).astype(BF16)


def kernel(
    sizes, tile,
    inputs_hbm, cotangent_hbm, filters_hbm, forward_hbm, wave_hbm, twiddle_hbm, backward_hbm,
    input_grad_ref, filter_grad_ref,
    inputs_ref, cotangent_ref, filters_ref, staged, staged_filter, late, early, spectrum, parts, result_narrow,
    result_wide, arrived, reduced_in, reduced_out, grad_in, forward_ref, wave_ref, twiddle_ref, backward_ref,
    load_sem, table_sem, send_sem, filter_send_sem, gather_send_sem, pass_send_sem, out_send_sem, reduce_send_sem,
    last_send_sem, late_sem, part_sem, gather_sem, pass_sem, out_sem, reduce_sem, last_sem,
):
    zs, groups, outer, inner = sizes
    blocks = 2 * zs
    half = inner // 2
    planes = groups // 2
    units = blocks // planes
    ctx = lax.axis_index("ctx")
    ch = lax.axis_index("ch")
    z, xl = ctx // 2, ctx % 2
    plane, core = ch // 2, ch % 2
    place = 2 * plane + xl

    loads = [
        pltpu.make_async_copy(cotangent_hbm, cotangent_ref, load_sem.at[0]),
        pltpu.make_async_copy(inputs_hbm, inputs_ref, load_sem.at[1]),
        pltpu.make_async_copy(filters_hbm, filters_ref, load_sem.at[2]),
    ]
    tables = [
        pltpu.make_async_copy(forward_hbm, forward_ref, table_sem.at[0]),
        pltpu.make_async_copy(wave_hbm, wave_ref, table_sem.at[1]),
        pltpu.make_async_copy(twiddle_hbm, twiddle_ref, table_sem.at[2]),
        pltpu.make_async_copy(backward_hbm, backward_ref, table_sem.at[3]),
    ]
    for copy in loads:
        copy.start()

    def is_self(to_ctx, to_ch):
        return jnp.logical_and(to_ctx == ctx, to_ch == ch)

    def remote(src, dst, ssem, rsem, to_ctx, to_ch):
        return pltpu.make_async_remote_copy(
            src_ref=src, dst_ref=dst, send_sem=ssem, recv_sem=rsem,
            device_id={"ctx": to_ctx, "ch": to_ch}, device_id_type=pl.DeviceIdType.MESH,
        )

    def start(src, dst, ssem, rsem, to_ctx, to_ch):
        own = is_self(to_ctx, to_ch)

        @pl.when(own)
        def _():
            pltpu.make_async_copy(src, dst, rsem).start()

        @pl.when(jnp.logical_not(own))
        def _():
            remote(src, dst, ssem, rsem, to_ctx, to_ch).start()

    def landed(ref, sem):
        pltpu.make_async_copy(ref, ref, sem).wait()

    def left(ref, number, own, sem):
        @pl.when(own)
        def _():
            landed(ref.at[pl.ds(0, number - 1)], sem)

        @pl.when(jnp.logical_not(own))
        def _():
            landed(ref.at[pl.ds(0, number)], sem)

    barrier = pltpu.get_barrier_semaphore()

    def greet(to_ctx, to_ch):
        @pl.when(jnp.logical_not(is_self(to_ctx, to_ch)))
        def _():
            pl.semaphore_signal(
                barrier, inc=1, device_id={"ctx": to_ctx, "ch": to_ch}, device_id_type=pl.DeviceIdType.MESH
            )

    def greet_sources(j, carry):
        greet(j, 2 * plane + xl)
        return carry

    def greet_plane(q, carry):
        greet(2 * z + q % 2, 2 * (q // 2) + core)
        return carry

    lax.fori_loop(0, blocks, greet_sources, 0)
    lax.fori_loop(0, groups, greet_plane, 0)
    for side in range(2):
        greet(2 * ch + side, 2 * (ctx % planes) + 1)

    count = zs * ROWS
    row = lax.broadcasted_iota(jnp.int32, (count, count), 0)
    col = lax.broadcasted_iota(jnp.int32, (count, count), 1)
    regroup = jnp.logical_and(row // ROWS == col % zs, row % ROWS == col // zs).astype(F32).astype(BF16)
    ungroup = jnp.logical_and(row % zs == col // ROWS, row // zs == col % ROWS).astype(F32).astype(BF16)

    def stage(value):
        stacked = jnp.concatenate([value[:, a * inner:(a + 1) * inner] for a in range(ROWS)], axis=0)
        return dot(regroup, stacked.astype(BF16)).astype(BF16).reshape(zs, ROWS, inner)

    loads[0].wait()
    staged[0] = stage(cotangent_ref[...].astype(F32))
    loads[1].wait()
    staged[1] = stage(inputs_ref[...].astype(F32))
    loads[2].wait()

    @pl.when(ch == z)
    def _():
        staged_filter[...] = stage(filters_ref[...])

    for copy in tables:
        copy.start()

    own_chip = xl == core
    expected = 2 * zs - own_chip.astype(jnp.int32) + groups - 1
    own_last = jnp.logical_and(ch == z, plane == ctx % planes)
    expected = expected + core * (units - own_last.astype(jnp.int32))
    pl.semaphore_wait(barrier, expected)

    def order(i):
        k = zs - 1 - i
        step = (k + 1) // 2
        off = jnp.where(k % 2 == 1, step, zs - step)
        return (z + off) % zs

    def rows(c):
        def args(i):
            f = order(i)
            return staged.at[c, f], late.at[ctx], send_sem.at[c], late_sem, 2 * f + core, 2 * plane + c
        return args

    def filter_rows(i):
        f = order(i)
        return staged_filter.at[f], early.at[ctx], filter_send_sem, part_sem, 2 * f + core, 2 * plane

    def each(number, *many):
        def body(i, carry):
            for args in many:
                start(*args(i))
            return carry
        lax.fori_loop(0, number, body, 0)

    @pl.when(ch == z)
    def _():
        each(zs, filter_rows)

    each(zs, rows(0))
    each(zs, rows(1))

    def gather_rows(k):
        q = (place + 1 + k) % groups
        block = early.at[pl.ds(2 * place, 2)]
        return block, block, gather_send_sem, gather_sem, 2 * z + q % 2, 2 * (q // 2)

    to_partner = (late, early, pass_send_sem, pass_sem, ctx, 2 * plane + 1)

    @pl.when(core == 0)
    def _():
        landed(early.at[pl.ds(2 * place, 2)], part_sem)
        each(groups - 1, gather_rows)
        landed(early.at[pl.ds(0, blocks - 2)], gather_sem)

    @pl.when(core == 1)
    def _():
        landed(early, pass_sem)

    for copy in tables[:3]:
        copy.wait()

    def turn(real, imag, rows_at):
        cosine = twiddle_ref[rows_at, :inner]
        sine = twiddle_ref[rows_at, inner:]
        return real * cosine - imag * sine, real * sine + imag * cosine

    def outer_transform(source, k, rows_at):
        both_parts = dot(forward_ref[k], source[...].reshape(outer, inner))
        real = both_parts[:tile] + both_parts[2 * tile:3 * tile]
        imag = both_parts[tile:2 * tile] + both_parts[3 * tile:]
        return turn(real, imag, rows_at)

    def inner_transform(real, imag):
        high, low = halves(jnp.concatenate([real, imag], axis=1))
        total = dot(jnp.concatenate([high, low], axis=0), wave_ref[:2 * inner])
        return total[:tile] + total[tile:] + dot(high, wave_ref[2 * inner:])

    def early_pass(k, carry):
        rows_at = pl.ds(pl.multiple_of(k * tile, tile), tile)
        spectrum[rows_at, :] = inner_transform(*outer_transform(early, k, rows_at))
        return carry

    steps = outer // tile
    lax.fori_loop(0, steps, early_pass, 0)

    landed(late, late_sem)

    @pl.when(core == 0)
    def _():
        remote(*to_partner).start()

    sign = (1 - 2 * core).astype(F32)

    def late_pass(k, carry):
        rows_at = pl.ds(pl.multiple_of(k * tile, tile), tile)
        other = inner_transform(*outer_transform(late, k, rows_at))
        mine = spectrum[rows_at, :]
        real_a, imag_a = mine[:, :inner], mine[:, inner:]
        real_b, imag_b = other[:, :inner], other[:, inner:]
        real = real_a * real_b + imag_a * imag_b
        imag = (imag_a * real_b - real_a * imag_b) * sign
        back = inner_transform(real, imag)
        real, imag = turn(back[:, :inner], back[:, inner:], rows_at)
        lower_at = pl.ds(pl.multiple_of(outer + k * tile, tile), tile)
        parts[0, rows_at, :], parts[1, rows_at, :] = halves(real)
        parts[0, lower_at, :], parts[1, lower_at, :] = halves(imag)
        return carry

    lax.fori_loop(0, steps, late_pass, 0)
    tables[3].wait()

    def last_pass(k, put):
        table = backward_ref[k]
        total = dot(table, parts[0])
        put(k, total[:tile] + total[tile:] + dot(table[:tile], parts[1]))

    def put_narrow(k, total):
        per_tile = tile // ROWS
        result_narrow[k * per_tile:(k + 1) * per_tile] = total.astype(BF16).reshape(per_tile, ROWS, inner)

    def put_wide(k, total):
        per_tile = tile // (ROWS * planes)
        total = total.reshape(per_tile, planes, ROWS, inner)
        for p in range(planes):
            for side in range(2):
                result_wide[2 * p + side, k * per_tile:(k + 1) * per_tile] = total[
                    :, p, :, side * half:(side + 1) * half
                ]

    def out_rows(x):
        def args(i):
            j = 2 * order(i) + x
            return result_narrow.at[j], arrived.at[z], out_send_sem, out_sem, j, 2 * plane + xl
        return args

    def reduce_rows(k):
        q = (place + k) % groups
        return (
            result_wide.at[q], reduced_in.at[place], reduce_send_sem, reduce_sem,
            2 * z + q % 2, 2 * (q // 2) + 1,
        )

    def last_rows(i):
        return reduced_out.at[i], grad_in.at[xl], last_send_sem, last_sem, planes * i + plane, z

    @pl.when(core == 0)
    def _():
        for k in range(steps):
            last_pass(k, put_narrow)
        each(zs, out_rows(0), out_rows(1))

    @pl.when(core == 1)
    def _():
        for k in range(steps):
            last_pass(k, put_wide)
        each(groups, reduce_rows)
        landed(reduced_in, reduce_sem)
        total = reduced_in[0]
        for q in range(1, groups):
            total = total + reduced_in[q]
        reduced_out[...] = total
        each(units, last_rows)

    left(staged.at[0], zs, jnp.logical_and(own_chip, core == 0), send_sem.at[0])
    left(staged.at[1], zs, jnp.logical_and(own_chip, core == 1), send_sem.at[1])

    @pl.when(ch == z)
    def _():
        left(staged_filter, zs, jnp.logical_and(own_chip, core == 0), filter_send_sem)

    @pl.when(core == 0)
    def _():
        landed(early.at[pl.ds(0, blocks - 2)], gather_send_sem)
        remote(*to_partner).wait_send()

    landed(arrived, out_sem)
    spread = dot(ungroup, arrived[...].reshape(count, inner)).astype(BF16)
    for a in range(ROWS):
        input_grad_ref[:, a * inner:(a + 1) * inner] = spread[a * zs:(a + 1) * zs]
    landed(grad_in, last_sem)
    for a in range(ROWS):
        for side in range(2):
            at = a * inner + side * half
            filter_grad_ref[:, at:at + half] = grad_in[side, a:a + 1]

    @pl.when(core == 0)
    def _():
        left(result_narrow, blocks, xl == 0, out_send_sem)

    @pl.when(core == 1)
    def _():
        landed(result_wide.at[pl.ds(0, groups - 1)], reduce_send_sem)
        left(reduced_out, units, own_last, last_send_sem)


def shards(tables, inputs, cotangent, filters):
    zs = lax.axis_size("ctx") // 2
    groups = lax.axis_size("ch")
    rows, length = inputs.shape
    inner = length // ROWS
    blocks = 2 * zs
    units = 2 * blocks // groups
    outer = blocks * ROWS
    tile = min(outer, 512)
    assert rows == zs and groups == zs and filters.shape[0] == zs
    vmem = pl.BlockSpec(memory_space=pltpu.VMEM)
    hbm = pl.BlockSpec(memory_space=pltpu.HBM)
    dma = pltpu.SemaphoreType.DMA
    return pl.pallas_call(
        functools.partial(kernel, (zs, groups, outer, inner), tile),
        out_shape=(
            jax.ShapeDtypeStruct((rows, length), BF16),
            jax.ShapeDtypeStruct((1, length), F32),
        ),
        in_specs=[hbm] * 7,
        out_specs=(vmem, vmem),
        scratch_shapes=[
            pltpu.VMEM((rows, length), BF16),
            pltpu.VMEM((rows, length), BF16),
            pltpu.VMEM((rows, length), F32),
            pltpu.VMEM((2, zs, ROWS, inner), BF16),
            pltpu.VMEM((zs, ROWS, inner), BF16),
            pltpu.VMEM((blocks, ROWS, inner), BF16),
            pltpu.VMEM((blocks, ROWS, inner), BF16),
            pltpu.VMEM((outer, 2 * inner), F32),
            pltpu.VMEM((2, 2 * outer, inner), BF16),
            pltpu.VMEM((blocks, ROWS, inner), BF16),
            pltpu.VMEM((groups, units, ROWS, inner // 2), F32),
            pltpu.VMEM((zs, ROWS, inner), BF16),
            pltpu.VMEM((groups, units, ROWS, inner // 2), F32),
            pltpu.VMEM((units, ROWS, inner // 2), F32),
            pltpu.VMEM((2, ROWS, inner // 2), F32),
            *[pltpu.VMEM(table.shape, table.dtype) for table in tables],
            dma((3,)), dma((4,)), dma((2,)), *[dma] * 13,
        ],
        compiler_params=pltpu.CompilerParams(
            collective_id=0, has_side_effects=True, vmem_limit_bytes=64 * 1024 * 1024
        ),
    )(inputs, cotangent, filters, *tables)


def solution(mesh):
    blocks = mesh.shape["ctx"]
    inner = 256
    outer = blocks * ROWS
    tables = make_tables(outer, inner, min(outer, 512))

    def whole(inputs, cotangent, filters):
        body = functools.partial(shards, tuple(jnp.asarray(table) for table in tables))
        return jax.shard_map(
            body,
            mesh=mesh,
            in_specs=(P("ch", "ctx"), P("ch", "ctx"), P(None, "ctx")),
            out_specs=(P("ch", "ctx"), P("ch", "ctx")),
            check_vma=False,
        )(inputs, cotangent, filters)

    return whole
```

time: 58.3 us -> 60.7 us (1.041)
  Pallas kernels: 54.6 us -> 56.6 us
    pallas_call x1, Pallas kernels: 54.6 us -> 56.6 us  [shards(): pl.pallas_call(functools.partial(kernel, (zs, groups, outer, inner), tile...]
where the time goes in v3:
time: 60.7 us; the launch traced here: 60.1 us
  Pallas kernels  56.6 us (93%)
  local copies, waits for them, and re-layouts  2.89 us (5%)
  between operations  0.64 us (1%)
    pallas_call x1, Pallas kernels, shards(): pl.pallas_call(functools.partial(kernel, (zs, groups, outer, inner), tile...  56.6 us
    unnamed x2, local copies, waits for them, and re-layouts  2.89 us

profile of v3, /device:TPU:6, one launch (start us, length us, event | category | flops | bytes accessed | tf_op | source)
XLA Modules:
  0.0 60.1 jit_solution(10874920346852586356)
XLA Ops:
  0.6 56.6 %shard_map.86 = (bf16[16,4096]{1,0:T(8,128)(2,1)}, f32[1,4096]{1,0:T(1,128)}) custom-call(bf16[16,4096]{1,0:T(8,128)(2,1)} %inputs_hbm.1, bf16[16,4096]{1,0:T(8,128)(2,1)} %cotangent_hbm.1, f32[16,4096]{1,0:T(8,128)} %filters_hbm.1, bf16[1,2048,512]{2,1,0:T(8,128)(2,1)} %constant.8.clone.forward_hbm, bf16[1024,512]{1,0:T(8,128)(2,1)} %constant.9.clone.wave_hbm, ...), custom_call_target="tpu_custom_call" | custom-call | tf_op jit(solution)/shard_map/pallas_call | solution.py:373
  57.2 1.6 %copy.11 = bf16[16,4096]{1,0:T(8,128)(2,1)} copy(bf16[16,4096]{1,0:T(8,128)(2,1)} %get-tuple-element.4) | data formatting | bytes 262144
  58.8 1.3 %copy.12 = f32[1,4096]{1,0:T(1,128)} copy(f32[1,4096]{1,0:T(1,128)} %get-tuple-element.5) | data formatting | bytes 32768

commit v4 on v3

--- a/solution.py
+++ b/solution.py
@@ -60,16 +60,13 @@
     sizes, tile,
     inputs_hbm, cotangent_hbm, filters_hbm, forward_hbm, wave_hbm, twiddle_hbm, backward_hbm,
     input_grad_ref, filter_grad_ref,
-    inputs_ref, cotangent_ref, filters_ref, staged, staged_filter, late, early, spectrum, parts, result_narrow,
-    result_wide, arrived, reduced_in, reduced_out, grad_in, forward_ref, wave_ref, twiddle_ref, backward_ref,
-    load_sem, table_sem, send_sem, filter_send_sem, gather_send_sem, pass_send_sem, out_send_sem, reduce_send_sem,
-    last_send_sem, late_sem, part_sem, gather_sem, pass_sem, out_sem, reduce_sem, last_sem,
+    inputs_ref, cotangent_ref, filters_ref, staged, staged_filter, early, late, spectrum, parts, result, arrived,
+    forward_ref, wave_ref, twiddle_ref, backward_ref,
+    load_sem, table_sem, send_sem, data_sem, out_sem, filter_send_sem, gather_send_sem, pass_send_sem,
+    result_send_sem, part_sem, gather_sem, pass_sem,
 ):
     zs, groups, outer, inner = sizes
     blocks = 2 * zs
-    half = inner // 2
-    planes = groups // 2
-    units = blocks // planes
     ctx = lax.axis_index("ctx")
     ch = lax.axis_index("ch")
     z, xl = ctx // 2, ctx % 2
@@ -131,18 +128,24 @@
                 barrier, inc=1, device_id={"ctx": to_ctx, "ch": to_ch}, device_id_type=pl.DeviceIdType.MESH
             )
 
-    def greet_sources(j, carry):
-        greet(j, 2 * plane + xl)
+    def greet_sources(k, carry):
+        greet((ctx + zs + k) % blocks, 2 * plane + xl)
+        return carry
+
+    def greet_ctx(g, carry):
+        greet(ctx, g)
         return carry
 
     def greet_plane(q, carry):
-        greet(2 * z + q % 2, 2 * (q // 2) + core)
+        greet(2 * z + q % 2, 2 * (q // 2))
         return carry
 
     lax.fori_loop(0, blocks, greet_sources, 0)
-    lax.fori_loop(0, groups, greet_plane, 0)
-    for side in range(2):
-        greet(2 * ch + side, 2 * (ctx % planes) + 1)
+    lax.fori_loop(0, groups, greet_ctx, 0)
+
+    @pl.when(core == 0)
+    def _():
+        lax.fori_loop(0, groups, greet_plane, 0)
 
     count = zs * ROWS
     row = lax.broadcasted_iota(jnp.int32, (count, count), 0)
@@ -168,9 +171,7 @@
         copy.start()
 
     own_chip = xl == core
-    expected = 2 * zs - own_chip.astype(jnp.int32) + groups - 1
-    own_last = jnp.logical_and(ch == z, plane == ctx % planes)
-    expected = expected + core * (units - own_last.astype(jnp.int32))
+    expected = 2 * zs - own_chip.astype(jnp.int32) + (groups - 1) * (2 - core)
     pl.semaphore_wait(barrier, expected)
 
     def order(i):
@@ -179,42 +180,48 @@
         off = jnp.where(k % 2 == 1, step, zs - step)
         return (z + off) % zs
 
-    def rows(c):
+    def rows(c, target):
         def args(i):
             f = order(i)
-            return staged.at[c, f], late.at[ctx], send_sem.at[c], late_sem, 2 * f + core, 2 * plane + c
+            return staged.at[c, f], target.at[ctx], send_sem.at[c], data_sem.at[c], 2 * f + core, 2 * plane + c
         return args
 
     def filter_rows(i):
         f = order(i)
-        return staged_filter.at[f], early.at[ctx], filter_send_sem, part_sem, 2 * f + core, 2 * plane
-
-    def each(number, *many):
+        return staged_filter.at[f], late.at[ctx], filter_send_sem, part_sem, 2 * f + core, 2 * plane
+
+    def each(first, number, *many):
         def body(i, carry):
             for args in many:
                 start(*args(i))
             return carry
-        lax.fori_loop(0, number, body, 0)
+        lax.fori_loop(first, number, body, 0)
 
     @pl.when(ch == z)
     def _():
-        each(zs, filter_rows)
-
-    each(zs, rows(0))
-    each(zs, rows(1))
+        each(0, zs, filter_rows)
+
+    each(0, zs, rows(0, early))
+    each(0, zs // 2, rows(1, late))
 
     def gather_rows(k):
         q = (place + 1 + k) % groups
-        block = early.at[pl.ds(2 * place, 2)]
+        block = late.at[pl.ds(2 * place, 2)]
         return block, block, gather_send_sem, gather_sem, 2 * z + q % 2, 2 * (q // 2)
 
-    to_partner = (late, early, pass_send_sem, pass_sem, ctx, 2 * plane + 1)
-
-    @pl.when(core == 0)
-    def _():
-        landed(early.at[pl.ds(2 * place, 2)], part_sem)
-        each(groups - 1, gather_rows)
-        landed(early.at[pl.ds(0, blocks - 2)], gather_sem)
+    @pl.when(core == 0)
+    def _():
+        landed(late.at[pl.ds(2 * place, 2)], part_sem)
+        each(0, groups - 1, gather_rows)
+
+    each(zs // 2, zs, rows(1, late))
+
+    to_partner = (early, early, pass_send_sem, pass_sem, ctx, 2 * plane + 1)
+
+    @pl.when(core == 0)
+    def _():
+        landed(early, data_sem.at[0])
+        remote(*to_partner).start()
 
     @pl.when(core == 1)
     def _():
@@ -247,13 +254,13 @@
     steps = outer // tile
     lax.fori_loop(0, steps, early_pass, 0)
 
-    landed(late, late_sem)
-
-    @pl.when(core == 0)
-    def _():
-        remote(*to_partner).start()
-
-    sign = (1 - 2 * core).astype(F32)
+    @pl.when(core == 0)
+    def _():
+        landed(late.at[pl.ds(0, blocks - 2)], gather_sem)
+
+    @pl.when(core == 1)
+    def _():
+        landed(late, data_sem.at[1])
 
     def late_pass(k, carry):
         rows_at = pl.ds(pl.multiple_of(k * tile, tile), tile)
@@ -262,7 +269,7 @@
         real_a, imag_a = mine[:, :inner], mine[:, inner:]
         real_b, imag_b = other[:, :inner], other[:, inner:]
         real = real_a * real_b + imag_a * imag_b
-        imag = (imag_a * real_b - real_a * imag_b) * sign
+        imag = real_a * imag_b - imag_a * real_b
         back = inner_transform(real, imag)
         real, imag = turn(back[:, :inner], back[:, inner:], rows_at)
         lower_at = pl.ds(pl.multiple_of(outer + k * tile, tile), tile)
@@ -273,57 +280,23 @@
     lax.fori_loop(0, steps, late_pass, 0)
     tables[3].wait()
 
-    def last_pass(k, put):
+    per_tile = tile // ROWS
+    for k in range(steps):
         table = backward_ref[k]
         total = dot(table, parts[0])
-        put(k, total[:tile] + total[tile:] + dot(table[:tile], parts[1]))
-
-    def put_narrow(k, total):
-        per_tile = tile // ROWS
-        result_narrow[k * per_tile:(k + 1) * per_tile] = total.astype(BF16).reshape(per_tile, ROWS, inner)
-
-    def put_wide(k, total):
-        per_tile = tile // (ROWS * planes)
-        total = total.reshape(per_tile, planes, ROWS, inner)
-        for p in range(planes):
-            for side in range(2):
-                result_wide[2 * p + side, k * per_tile:(k + 1) * per_tile] = total[
-                    :, p, :, side * half:(side + 1) * half
-                ]
-
-    def out_rows(x):
+        total = total[:tile] + total[tile:] + dot(table[:tile], parts[1])
+        result[k * per_tile:(k + 1) * per_tile] = total.astype(BF16).reshape(per_tile, ROWS, inner)
+
+    slot = jnp.where(core == 0, z, place)
+    owner = jnp.where(core == 0, 2 * plane + xl, z)
+
+    def result_rows(x):
         def args(i):
             j = 2 * order(i) + x
-            return result_narrow.at[j], arrived.at[z], out_send_sem, out_sem, j, 2 * plane + xl
+            return result.at[j], arrived.at[core, slot], result_send_sem, out_sem.at[core], j, owner
         return args
 
-    def reduce_rows(k):
-        q = (place + k) % groups
-        return (
-            result_wide.at[q], reduced_in.at[place], reduce_send_sem, reduce_sem,
-            2 * z + q % 2, 2 * (q // 2) + 1,
-        )
-
-    def last_rows(i):
-        return reduced_out.at[i], grad_in.at[xl], last_send_sem, last_sem, planes * i + plane, z
-
-    @pl.when(core == 0)
-    def _():
-        for k in range(steps):
-            last_pass(k, put_narrow)
-        each(zs, out_rows(0), out_rows(1))
-
-    @pl.when(core == 1)
-    def _():
-        for k in range(steps):
-            last_pass(k, put_wide)
-        each(groups, reduce_rows)
-        landed(reduced_in, reduce_sem)
-        total = reduced_in[0]
-        for q in range(1, groups):
-            total = total + reduced_in[q]
-        reduced_out[...] = total
-        each(units, last_rows)
+    each(0, zs, result_rows(0), result_rows(1))
 
     left(staged.at[0], zs, jnp.logical_and(own_chip, core == 0), send_sem.at[0])
     left(staged.at[1], zs, jnp.logical_and(own_chip, core == 1), send_sem.at[1])
@@ -334,27 +307,18 @@
 
     @pl.when(core == 0)
     def _():
-        landed(early.at[pl.ds(0, blocks - 2)], gather_send_sem)
+        landed(late.at[pl.ds(0, blocks - 2)], gather_send_sem)
         remote(*to_partner).wait_send()
 
-    landed(arrived, out_sem)
-    spread = dot(ungroup, arrived[...].reshape(count, inner)).astype(BF16)
+    landed(arrived.at[0], out_sem.at[0])
+    spread = dot(ungroup, arrived[0].reshape(count, inner)).astype(BF16)
     for a in range(ROWS):
         input_grad_ref[:, a * inner:(a + 1) * inner] = spread[a * zs:(a + 1) * zs]
-    landed(grad_in, last_sem)
+    landed(arrived.at[1], out_sem.at[1])
+    total = jnp.sum(arrived[1].astype(F32), axis=0)
     for a in range(ROWS):
-        for side in range(2):
-            at = a * inner + side * half
-            filter_grad_ref[:, at:at + half] = grad_in[side, a:a + 1]
-
-    @pl.when(core == 0)
-    def _():
-        left(result_narrow, blocks, xl == 0, out_send_sem)
-
-    @pl.when(core == 1)
-    def _():
-        landed(result_wide.at[pl.ds(0, groups - 1)], reduce_send_sem)
-        left(reduced_out, units, own_last, last_send_sem)
+        filter_grad_ref[:, a * inner:(a + 1) * inner] = total[a:a + 1]
+    left(result, blocks, owner == ch, result_send_sem)
 
 
 def shards(tables, inputs, cotangent, filters):
@@ -363,7 +327,6 @@
     rows, length = inputs.shape
     inner = length // ROWS
     blocks = 2 * zs
-    units = 2 * blocks // groups
     outer = blocks * ROWS
     tile = min(outer, 512)
     assert rows == zs and groups == zs and filters.shape[0] == zs
@@ -389,13 +352,9 @@
             pltpu.VMEM((outer, 2 * inner), F32),
             pltpu.VMEM((2, 2 * outer, inner), BF16),
             pltpu.VMEM((blocks, ROWS, inner), BF16),
-            pltpu.VMEM((groups, units, ROWS, inner // 2), F32),
-            pltpu.VMEM((zs, ROWS, inner), BF16),
-            pltpu.VMEM((groups, units, ROWS, inner // 2), F32),
-            pltpu.VMEM((units, ROWS, inner // 2), F32),
-            pltpu.VMEM((2, ROWS, inner // 2), F32),
+            pltpu.VMEM((2, groups, ROWS, inner), BF16),
             *[pltpu.VMEM(table.shape, table.dtype) for table in tables],
-            dma((3,)), dma((4,)), dma((2,)), *[dma] * 13,
+            dma((3,)), dma((4,)), dma((2,)), dma((2,)), dma((2,)), *[dma] * 7,
         ],
         compiler_params=pltpu.CompilerParams(
             collective_id=0, has_side_effects=True, vmem_limit_bytes=64 * 1024 * 1024

time: 60.7 us -> 59.6 us (0.982)
  the two profiles are of different devices: /device:TPU:6 before, /device:TPU:1 now
where the time goes in v4:
time: 59.6 us; the launch traced here: 59.4 us
  Pallas kernels  55.9 us (94%)
  local copies, waits for them, and re-layouts  2.89 us (5%)
  between operations  0.64 us (1%)
    pallas_call x1, Pallas kernels, shards(): pl.pallas_call(functools.partial(kernel, (zs, groups, outer, inner), tile...  55.9 us
    unnamed x2, local copies, waits for them, and re-layouts  2.89 us

profile of v4, /device:TPU:1, one launch (start us, length us, event | category | flops | bytes accessed | tf_op | source)
XLA Modules:
  0.0 59.4 jit_solution(175532487708720325)
XLA Ops:
  0.6 55.9 %shard_map.86 = (bf16[16,4096]{1,0:T(8,128)(2,1)}, f32[1,4096]{1,0:T(1,128)}) custom-call(bf16[16,4096]{1,0:T(8,128)(2,1)} %inputs_hbm.1, bf16[16,4096]{1,0:T(8,128)(2,1)} %cotangent_hbm.1, f32[16,4096]{1,0:T(8,128)} %filters_hbm.1, bf16[1,2048,512]{2,1,0:T(8,128)(2,1)} %constant.8.clone.forward_hbm, bf16[1024,512]{1,0:T(8,128)(2,1)} %constant.9.clone.wave_hbm, ...), custom_call_target="tpu_custom_call" | custom-call | tf_op jit(solution)/shard_map/pallas_call | solution.py:336
  56.5 1.6 %copy.11 = bf16[16,4096]{1,0:T(8,128)(2,1)} copy(bf16[16,4096]{1,0:T(8,128)(2,1)} %get-tuple-element.4) | data formatting | bytes 262144
  58.1 1.3 %copy.12 = f32[1,4096]{1,0:T(1,128)} copy(f32[1,4096]{1,0:T(1,128)} %get-tuple-element.5) | data formatting | bytes 32768

commit v5 on v4

--- a/solution.py
+++ b/solution.py
@@ -60,13 +60,16 @@
     sizes, tile,
     inputs_hbm, cotangent_hbm, filters_hbm, forward_hbm, wave_hbm, twiddle_hbm, backward_hbm,
     input_grad_ref, filter_grad_ref,
-    inputs_ref, cotangent_ref, filters_ref, staged, staged_filter, early, late, spectrum, parts, result, arrived,
-    forward_ref, wave_ref, twiddle_ref, backward_ref,
-    load_sem, table_sem, send_sem, data_sem, out_sem, filter_send_sem, gather_send_sem, pass_send_sem,
-    result_send_sem, part_sem, gather_sem, pass_sem,
+    inputs_ref, cotangent_ref, filters_ref, staged, staged_filter, early, late, spectrum, parts, result, result_tiles,
+    arrived, reduced_in, reduced_out, grad_in, forward_ref, wave_ref, twiddle_ref, backward_ref,
+    load_sem, table_sem, send_sem, data_sem, filter_send_sem, gather_send_sem, pass_send_sem, out_send_sem,
+    reduce_send_sem, last_send_sem, part_sem, gather_sem, pass_sem, out_sem, reduce_sem, last_sem,
 ):
     zs, groups, outer, inner = sizes
     blocks = 2 * zs
+    half = inner // 2
+    planes = groups // 2
+    units = blocks // planes
     ctx = lax.axis_index("ctx")
     ch = lax.axis_index("ch")
     z, xl = ctx // 2, ctx % 2
@@ -137,15 +140,13 @@
         return carry
 
     def greet_plane(q, carry):
-        greet(2 * z + q % 2, 2 * (q // 2))
+        greet(2 * z + q % 2, 2 * (q // 2) + core)
         return carry
 
     lax.fori_loop(0, blocks, greet_sources, 0)
     lax.fori_loop(0, groups, greet_ctx, 0)
 
-    @pl.when(core == 0)
-    def _():
-        lax.fori_loop(0, groups, greet_plane, 0)
+    lax.fori_loop(0, groups, greet_plane, 0)
 
     count = zs * ROWS
     row = lax.broadcasted_iota(jnp.int32, (count, count), 0)
@@ -171,7 +172,7 @@
         copy.start()
 
     own_chip = xl == core
-    expected = 2 * zs - own_chip.astype(jnp.int32) + (groups - 1) * (2 - core)
+    expected = 2 * zs - own_chip.astype(jnp.int32) + 2 * (groups - 1)
     pl.semaphore_wait(barrier, expected)
 
     def order(i):
@@ -202,7 +203,7 @@
         each(0, zs, filter_rows)
 
     each(0, zs, rows(0, early))
-    each(0, zs // 2, rows(1, late))
+    each(0, zs, rows(1, late))
 
     def gather_rows(k):
         q = (place + 1 + k) % groups
@@ -214,8 +215,6 @@
         landed(late.at[pl.ds(2 * place, 2)], part_sem)
         each(0, groups - 1, gather_rows)
 
-    each(zs // 2, zs, rows(1, late))
-
     to_partner = (early, early, pass_send_sem, pass_sem, ctx, 2 * plane + 1)
 
     @pl.when(core == 0)
@@ -236,23 +235,24 @@
         return real * cosine - imag * sine, real * sine + imag * cosine
 
     def outer_transform(source, k, rows_at):
-        both_parts = dot(forward_ref[k], source[...].reshape(outer, inner))
-        real = both_parts[:tile] + both_parts[2 * tile:3 * tile]
-        imag = both_parts[tile:2 * tile] + both_parts[3 * tile:]
-        return turn(real, imag, rows_at)
+        table = forward_ref[k]
+        flat = source[...].reshape(outer, inner)
+        both_parts = dot(
+            jnp.concatenate([table[:2 * tile], table[2 * tile:]], axis=1), jnp.concatenate([flat, flat], axis=0)
+        )
+        return turn(both_parts[:tile], both_parts[tile:], rows_at)
 
     def inner_transform(real, imag):
         high, low = halves(jnp.concatenate([real, imag], axis=1))
-        total = dot(jnp.concatenate([high, low], axis=0), wave_ref[:2 * inner])
-        return total[:tile] + total[tile:] + dot(high, wave_ref[2 * inner:])
-
-    def early_pass(k, carry):
-        rows_at = pl.ds(pl.multiple_of(k * tile, tile), tile)
+        wave_high, wave_low = wave_ref[:2 * inner], wave_ref[2 * inner:]
+        return dot(
+            jnp.concatenate([high, low, high], axis=1), jnp.concatenate([wave_high, wave_high, wave_low], axis=0)
+        )
+
+    steps = outer // tile
+    for k in range(steps):
+        rows_at = pl.ds(k * tile, tile)
         spectrum[rows_at, :] = inner_transform(*outer_transform(early, k, rows_at))
-        return carry
-
-    steps = outer // tile
-    lax.fori_loop(0, steps, early_pass, 0)
 
     @pl.when(core == 0)
     def _():
@@ -262,8 +262,8 @@
     def _():
         landed(late, data_sem.at[1])
 
-    def late_pass(k, carry):
-        rows_at = pl.ds(pl.multiple_of(k * tile, tile), tile)
+    for k in range(steps):
+        rows_at = pl.ds(k * tile, tile)
         other = inner_transform(*outer_transform(late, k, rows_at))
         mine = spectrum[rows_at, :]
         real_a, imag_a = mine[:, :inner], mine[:, inner:]
@@ -272,31 +272,57 @@
         imag = real_a * imag_b - imag_a * real_b
         back = inner_transform(real, imag)
         real, imag = turn(back[:, :inner], back[:, inner:], rows_at)
-        lower_at = pl.ds(pl.multiple_of(outer + k * tile, tile), tile)
+        lower_at = pl.ds(outer + k * tile, tile)
         parts[0, rows_at, :], parts[1, rows_at, :] = halves(real)
         parts[0, lower_at, :], parts[1, lower_at, :] = halves(imag)
-        return carry
-
-    lax.fori_loop(0, steps, late_pass, 0)
     tables[3].wait()
 
     per_tile = tile // ROWS
     for k in range(steps):
         table = backward_ref[k]
-        total = dot(table, parts[0])
-        total = total[:tile] + total[tile:] + dot(table[:tile], parts[1])
-        result[k * per_tile:(k + 1) * per_tile] = total.astype(BF16).reshape(per_tile, ROWS, inner)
-
-    slot = jnp.where(core == 0, z, place)
-    owner = jnp.where(core == 0, 2 * plane + xl, z)
-
-    def result_rows(x):
+        high, low = parts[0], parts[1]
+        total = dot(
+            jnp.concatenate([table[:tile], table[:tile], table[tile:]], axis=1),
+            jnp.concatenate([high, low, high], axis=0),
+        ).astype(BF16)
+        total = total.reshape(per_tile, ROWS, inner)
+        result[k * per_tile:(k + 1) * per_tile] = total
+        for i in range(per_tile):
+            unit, p = divmod(k * per_tile + i, planes)
+            for side in range(2):
+                result_tiles[2 * p + side, unit] = total[i, :, side * half:(side + 1) * half]
+
+    def out_rows(x):
         def args(i):
             j = 2 * order(i) + x
-            return result.at[j], arrived.at[core, slot], result_send_sem, out_sem.at[core], j, owner
+            return result.at[j], arrived.at[z], out_send_sem, out_sem, j, 2 * plane + xl
         return args
 
-    each(0, zs, result_rows(0), result_rows(1))
+    def reduce_rows(k):
+        q = (place + 1 + k) % groups
+        return (
+            result_tiles.at[q], reduced_in.at[place], reduce_send_sem, reduce_sem,
+            2 * z + q % 2, 2 * (q // 2) + 1,
+        )
+
+    def last_rows(i):
+        return reduced_out.at[i], grad_in.at[xl], last_send_sem, last_sem, planes * i + plane, z
+
+    own_last = jnp.logical_and(ch == z, plane == ctx % planes)
+
+    @pl.when(core == 0)
+    def _():
+        each(0, zs, out_rows(0), out_rows(1))
+
+    @pl.when(core == 1)
+    def _():
+        each(0, groups, reduce_rows)
+        landed(reduced_in, reduce_sem)
+        total = reduced_in[0].astype(F32)
+        for q in range(1, groups):
+            total = total + reduced_in[q].astype(F32)
+        reduced_out[...] = total
+        each(0, units, last_rows)
 
     left(staged.at[0], zs, jnp.logical_and(own_chip, core == 0), send_sem.at[0])
     left(staged.at[1], zs, jnp.logical_and(own_chip, core == 1), send_sem.at[1])
@@ -310,15 +336,24 @@
         landed(late.at[pl.ds(0, blocks - 2)], gather_send_sem)
         remote(*to_partner).wait_send()
 
-    landed(arrived.at[0], out_sem.at[0])
-    spread = dot(ungroup, arrived[0].reshape(count, inner)).astype(BF16)
+    landed(arrived, out_sem)
+    spread = dot(ungroup, arrived[...].reshape(count, inner)).astype(BF16)
     for a in range(ROWS):
         input_grad_ref[:, a * inner:(a + 1) * inner] = spread[a * zs:(a + 1) * zs]
-    landed(arrived.at[1], out_sem.at[1])
-    total = jnp.sum(arrived[1].astype(F32), axis=0)
+    landed(grad_in, last_sem)
     for a in range(ROWS):
-        filter_grad_ref[:, a * inner:(a + 1) * inner] = total[a:a + 1]
-    left(result, blocks, owner == ch, result_send_sem)
+        for side in range(2):
+            at = a * inner + side * half
+            filter_grad_ref[:, at:at + half] = grad_in[side, a:a + 1]
+
+    @pl.when(core == 0)
+    def _():
+        left(result, blocks, xl == 0, out_send_sem)
+
+    @pl.when(core == 1)
+    def _():
+        landed(result_tiles.at[pl.ds(0, groups - 1)], reduce_send_sem)
+        left(reduced_out, units, own_last, last_send_sem)
 
 
 def shards(tables, inputs, cotangent, filters):
@@ -327,8 +362,9 @@
     rows, length = inputs.shape
     inner = length // ROWS
     blocks = 2 * zs
+    units = 2 * blocks // groups
     outer = blocks * ROWS
-    tile = min(outer, 512)
+    tile = min(outer, 256)
     assert rows == zs and groups == zs and filters.shape[0] == zs
     vmem = pl.BlockSpec(memory_space=pltpu.VMEM)
     hbm = pl.BlockSpec(memory_space=pltpu.HBM)
@@ -352,9 +388,13 @@
             pltpu.VMEM((outer, 2 * inner), F32),
             pltpu.VMEM((2, 2 * outer, inner), BF16),
             pltpu.VMEM((blocks, ROWS, inner), BF16),
-            pltpu.VMEM((2, groups, ROWS, inner), BF16),
+            pltpu.VMEM((groups, units, ROWS, inner // 2), BF16),
+            pltpu.VMEM((zs, ROWS, inner), BF16),
+            pltpu.VMEM((groups, units, ROWS, inner // 2), BF16),
+            pltpu.VMEM((units, ROWS, inner // 2), F32),
+            pltpu.VMEM((2, ROWS, inner // 2), F32),
             *[pltpu.VMEM(table.shape, table.dtype) for table in tables],
-            dma((3,)), dma((4,)), dma((2,)), dma((2,)), dma((2,)), *[dma] * 7,
+            dma((3,)), dma((4,)), dma((2,)), dma((2,)), *[dma] * 12,
         ],
         compiler_params=pltpu.CompilerParams(
             collective_id=0, has_side_effects=True, vmem_limit_bytes=64 * 1024 * 1024
@@ -366,7 +406,7 @@
     blocks = mesh.shape["ctx"]
     inner = 256
     outer = blocks * ROWS
-    tables = make_tables(outer, inner, min(outer, 512))
+    tables = make_tables(outer, inner, min(outer, 256))
 
     def whole(inputs, cotangent, filters):
         body = functools.partial(shards, tuple(jnp.asarray(table) for table in tables))

time: 59.6 us -> 54.3 us (0.911)
  the two profiles are of different devices: /device:TPU:1 before, /device:TPU:6 now
where the time goes in v5:
time: 54.3 us; the launch traced here: 53.7 us
  Pallas kernels  50.1 us (92%)
  local copies, waits for them, and re-layouts  2.89 us (5%)
  between operations  0.64 us (1%)
    pallas_call x1, Pallas kernels, shards(): pl.pallas_call(functools.partial(kernel, (zs, groups, outer, inner), tile...  50.1 us
    unnamed x2, local copies, waits for them, and re-layouts  2.89 us

profile of v5, /device:TPU:6, one launch (start us, length us, event | category | flops | bytes accessed | tf_op | source)
XLA Modules:
  0.0 53.7 jit_solution(17540850404026686855)
XLA Ops:
  0.6 50.1 %shard_map.86 = (bf16[16,4096]{1,0:T(8,128)(2,1)}, f32[1,4096]{1,0:T(1,128)}) custom-call(bf16[16,4096]{1,0:T(8,128)(2,1)} %inputs_hbm.1, bf16[16,4096]{1,0:T(8,128)(2,1)} %cotangent_hbm.1, f32[16,4096]{1,0:T(8,128)} %filters_hbm.1, bf16[2,1024,512]{2,1,0:T(8,128)(2,1)} %constant.8.clone.forward_hbm, bf16[1024,512]{1,0:T(8,128)(2,1)} %constant.9.clone.wave_hbm, ...), custom_call_target="tpu_custom_call" | custom-call | tf_op jit(solution)/shard_map/pallas_call | solution.py:372
  50.8 1.6 %copy.11 = bf16[16,4096]{1,0:T(8,128)(2,1)} copy(bf16[16,4096]{1,0:T(8,128)(2,1)} %get-tuple-element.4) | data formatting | bytes 262144
  52.3 1.3 %copy.12 = f32[1,4096]{1,0:T(1,128)} copy(f32[1,4096]{1,0:T(1,128)} %get-tuple-element.5) | data formatting | bytes 32768

commit v6 on v5

--- a/solution.py
+++ b/solution.py
@@ -12,6 +12,7 @@
 
 ROWS = 16
 BF16 = jnp.bfloat16
+NEAR = (8, 7, -7, 4, 6, 5, -4, 3, -3, 2, -1, 0, -6, -5, -2, 1)
 F32 = jnp.float32
 
 
@@ -60,21 +61,19 @@
     sizes, tile,
     inputs_hbm, cotangent_hbm, filters_hbm, forward_hbm, wave_hbm, twiddle_hbm, backward_hbm,
     input_grad_ref, filter_grad_ref,
-    inputs_ref, cotangent_ref, filters_ref, staged, staged_filter, early, late, spectrum, parts, result, result_tiles,
+    inputs_ref, cotangent_ref, filters_ref, staged, staged_filter, gathered, spectrum, parts, result,
     arrived, reduced_in, reduced_out, grad_in, forward_ref, wave_ref, twiddle_ref, backward_ref,
     load_sem, table_sem, send_sem, data_sem, filter_send_sem, gather_send_sem, pass_send_sem, out_send_sem,
     reduce_send_sem, last_send_sem, part_sem, gather_sem, pass_sem, out_sem, reduce_sem, last_sem,
 ):
     zs, groups, outer, inner = sizes
     blocks = 2 * zs
-    half = inner // 2
-    planes = groups // 2
-    units = blocks // planes
     ctx = lax.axis_index("ctx")
     ch = lax.axis_index("ch")
-    z, xl = ctx // 2, ctx % 2
-    plane, core = ch // 2, ch % 2
+    z, xl = ctx >> 1, ctx & 1
+    plane, core = ch >> 1, ch & 1
     place = 2 * plane + xl
+    early, late = gathered.at[0], gathered.at[1]
 
     loads = [
         pltpu.make_async_copy(cotangent_hbm, cotangent_ref, load_sem.at[0]),
@@ -132,7 +131,7 @@
             )
 
     def greet_sources(k, carry):
-        greet((ctx + zs + k) % blocks, 2 * plane + xl)
+        greet((ctx + zs + k) & (blocks - 1), 2 * plane + xl)
         return carry
 
     def greet_ctx(g, carry):
@@ -140,7 +139,7 @@
         return carry
 
     def greet_plane(q, carry):
-        greet(2 * z + q % 2, 2 * (q // 2) + core)
+        greet(2 * z + (q & 1), (q & -2) + core)
         return carry
 
     lax.fori_loop(0, blocks, greet_sources, 0)
@@ -177,9 +176,8 @@
 
     def order(i):
         k = zs - 1 - i
-        step = (k + 1) // 2
-        off = jnp.where(k % 2 == 1, step, zs - step)
-        return (z + off) % zs
+        step = (k + 1) >> 1
+        return (z + jnp.where((k & 1) == 1, step, zs - step)) & (zs - 1)
 
     def rows(c, target):
         def args(i):
@@ -206,9 +204,9 @@
     each(0, zs, rows(1, late))
 
     def gather_rows(k):
-        q = (place + 1 + k) % groups
+        q = (place + 1 + k) & (groups - 1)
         block = late.at[pl.ds(2 * place, 2)]
-        return block, block, gather_send_sem, gather_sem, 2 * z + q % 2, 2 * (q // 2)
+        return block, block, gather_send_sem, gather_sem, 2 * z + (q & 1), q & -2
 
     @pl.when(core == 0)
     def _():
@@ -234,9 +232,9 @@
         sine = twiddle_ref[rows_at, inner:]
         return real * cosine - imag * sine, real * sine + imag * cosine
 
-    def outer_transform(source, k, rows_at):
+    def outer_transform(which, k, rows_at):
         table = forward_ref[k]
-        flat = source[...].reshape(outer, inner)
+        flat = gathered[which].reshape(outer, inner)
         both_parts = dot(
             jnp.concatenate([table[:2 * tile], table[2 * tile:]], axis=1), jnp.concatenate([flat, flat], axis=0)
         )
@@ -250,22 +248,26 @@
         )
 
     steps = outer // tile
+
+    def transform(which, carry):
+        @pl.when(jnp.logical_and(which == 1, core == 0))
+        def _():
+            landed(late.at[pl.ds(0, blocks - 2)], gather_sem)
+
+        @pl.when(jnp.logical_and(which == 1, core == 1))
+        def _():
+            landed(late, data_sem.at[1])
+
+        for k in range(steps):
+            rows_at = pl.ds(k * tile, tile)
+            spectrum[which, rows_at, :] = inner_transform(*outer_transform(which, k, rows_at))
+        return carry
+
+    lax.fori_loop(0, 2, transform, 0)
+
     for k in range(steps):
         rows_at = pl.ds(k * tile, tile)
-        spectrum[rows_at, :] = inner_transform(*outer_transform(early, k, rows_at))
-
-    @pl.when(core == 0)
-    def _():
-        landed(late.at[pl.ds(0, blocks - 2)], gather_sem)
-
-    @pl.when(core == 1)
-    def _():
-        landed(late, data_sem.at[1])
-
-    for k in range(steps):
-        rows_at = pl.ds(k * tile, tile)
-        other = inner_transform(*outer_transform(late, k, rows_at))
-        mine = spectrum[rows_at, :]
+        mine, other = spectrum[0, rows_at, :], spectrum[1, rows_at, :]
         real_a, imag_a = mine[:, :inner], mine[:, inner:]
         real_b, imag_b = other[:, :inner], other[:, inner:]
         real = real_a * real_b + imag_a * imag_b
@@ -287,10 +289,6 @@
         ).astype(BF16)
         total = total.reshape(per_tile, ROWS, inner)
         result[k * per_tile:(k + 1) * per_tile] = total
-        for i in range(per_tile):
-            unit, p = divmod(k * per_tile + i, planes)
-            for side in range(2):
-                result_tiles[2 * p + side, unit] = total[i, :, side * half:(side + 1) * half]
 
     def out_rows(x):
         def args(i):
@@ -298,17 +296,30 @@
             return result.at[j], arrived.at[z], out_send_sem, out_sem, j, 2 * plane + xl
         return args
 
+    def reduced_z(q):
+        if zs != len(NEAR):
+            return (z + q) & (zs - 1)
+        side_y = ((q >> 1) - (z >> 1)) & 3
+        side_x = ((q >> 3) + (z >> 3)) & 1
+        entry = 4 * side_y + 2 * side_x + (q & 1)
+        off = 0
+        for n, value in enumerate(NEAR):
+            off = jnp.where(entry == n, value % zs, off)
+        return (z + off) & (zs - 1)
+
     def reduce_rows(k):
-        q = (place + 1 + k) % groups
+        q = (place + 1 + k) & (groups - 1)
         return (
-            result_tiles.at[q], reduced_in.at[place], reduce_send_sem, reduce_sem,
-            2 * z + q % 2, 2 * (q // 2) + 1,
+            result.at[pl.ds(2 * reduced_z(q), 2)], reduced_in.at[place], reduce_send_sem, reduce_sem,
+            2 * z + (q & 1), (q & -2) + 1,
         )
 
+    last_z = reduced_z(place)
+
     def last_rows(i):
-        return reduced_out.at[i], grad_in.at[xl], last_send_sem, last_sem, planes * i + plane, z
-
-    own_last = jnp.logical_and(ch == z, plane == ctx % planes)
+        return reduced_out.at[i], grad_in, last_send_sem, last_sem, 2 * last_z + i, z
+
+    own_last = jnp.logical_and(ch == z, last_z == z)
 
     @pl.when(core == 0)
     def _():
@@ -322,7 +333,7 @@
         for q in range(1, groups):
             total = total + reduced_in[q].astype(F32)
         reduced_out[...] = total
-        each(0, units, last_rows)
+        each(0, 2, last_rows)
 
     left(staged.at[0], zs, jnp.logical_and(own_chip, core == 0), send_sem.at[0])
     left(staged.at[1], zs, jnp.logical_and(own_chip, core == 1), send_sem.at[1])
@@ -342,9 +353,7 @@
         input_grad_ref[:, a * inner:(a + 1) * inner] = spread[a * zs:(a + 1) * zs]
     landed(grad_in, last_sem)
     for a in range(ROWS):
-        for side in range(2):
-            at = a * inner + side * half
-            filter_grad_ref[:, at:at + half] = grad_in[side, a:a + 1]
+        filter_grad_ref[:, a * inner:(a + 1) * inner] = grad_in[a:a + 1]
 
     @pl.when(core == 0)
     def _():
@@ -352,8 +361,8 @@
 
     @pl.when(core == 1)
     def _():
-        landed(result_tiles.at[pl.ds(0, groups - 1)], reduce_send_sem)
-        left(reduced_out, units, own_last, last_send_sem)
+        landed(result.at[pl.ds(0, blocks - 2)], reduce_send_sem)
+        left(reduced_out, 2, own_last, last_send_sem)
 
 
 def shards(tables, inputs, cotangent, filters):
@@ -362,10 +371,9 @@
     rows, length = inputs.shape
     inner = length // ROWS
     blocks = 2 * zs
-    units = 2 * blocks // groups
     outer = blocks * ROWS
     tile = min(outer, 256)
-    assert rows == zs and groups == zs and filters.shape[0] == zs
+    assert zs & (zs - 1) == 0 and rows == zs and groups == zs and filters.shape[0] == zs
     vmem = pl.BlockSpec(memory_space=pltpu.VMEM)
     hbm = pl.BlockSpec(memory_space=pltpu.HBM)
     dma = pltpu.SemaphoreType.DMA
@@ -383,16 +391,14 @@
             pltpu.VMEM((rows, length), F32),
             pltpu.VMEM((2, zs, ROWS, inner), BF16),
             pltpu.VMEM((zs, ROWS, inner), BF16),
-            pltpu.VMEM((blocks, ROWS, inner), BF16),
-            pltpu.VMEM((blocks, ROWS, inner), BF16),
-            pltpu.VMEM((outer, 2 * inner), F32),
+            pltpu.VMEM((2, blocks, ROWS, inner), BF16),
+            pltpu.VMEM((2, outer, 2 * inner), F32),
             pltpu.VMEM((2, 2 * outer, inner), BF16),
             pltpu.VMEM((blocks, ROWS, inner), BF16),
-            pltpu.VMEM((groups, units, ROWS, inner // 2), BF16),
             pltpu.VMEM((zs, ROWS, inner), BF16),
-            pltpu.VMEM((groups, units, ROWS, inner // 2), BF16),
-            pltpu.VMEM((units, ROWS, inner // 2), F32),
-            pltpu.VMEM((2, ROWS, inner // 2), F32),
+            pltpu.VMEM((groups, 2, ROWS, inner), BF16),
+            pltpu.VMEM((2, ROWS, inner), F32),
+            pltpu.VMEM((ROWS, inner), F32),
             *[pltpu.VMEM(table.shape, table.dtype) for table in tables],
             dma((3,)), dma((4,)), dma((2,)), dma((2,)), *[dma] * 12,
         ],

time: 54.3 us -> 53.4 us (0.983)
  Pallas kernels: 50.1 us -> 49 us
    pallas_call x1, Pallas kernels: 50.1 us -> 49 us  [shards(): pl.pallas_call(functools.partial(kernel, (zs, groups, outer, inner), tile...]
where the time goes in v6:
time: 53.4 us; the launch traced here: 52.5 us
  Pallas kernels  49 us (92%)
  local copies, waits for them, and re-layouts  2.89 us (5%)
  between operations  0.64 us (1%)
    pallas_call x1, Pallas kernels, shards(): pl.pallas_call(functools.partial(kernel, (zs, groups, outer, inner), tile...  49 us
    unnamed x2, local copies, waits for them, and re-layouts  2.89 us

profile of v6, /device:TPU:6, one launch (start us, length us, event | category | flops | bytes accessed | tf_op | source)
XLA Modules:
  0.0 52.5 jit_solution(3185290177894874987)
XLA Ops:
  0.6 49.0 %shard_map.86 = (bf16[16,4096]{1,0:T(8,128)(2,1)}, f32[1,4096]{1,0:T(1,128)}) custom-call(bf16[16,4096]{1,0:T(8,128)(2,1)} %inputs_hbm.1, bf16[16,4096]{1,0:T(8,128)(2,1)} %cotangent_hbm.1, f32[16,4096]{1,0:T(8,128)} %filters_hbm.1, bf16[2,1024,512]{2,1,0:T(8,128)(2,1)} %constant.8.clone.forward_hbm, bf16[1024,512]{1,0:T(8,128)(2,1)} %constant.9.clone.wave_hbm, ...), custom_call_target="tpu_custom_call" | custom-call | tf_op jit(solution)/shard_map/pallas_call | solution.py:380
  49.6 1.6 %copy.11 = bf16[16,4096]{1,0:T(8,128)(2,1)} copy(bf16[16,4096]{1,0:T(8,128)(2,1)} %get-tuple-element.4) | data formatting | bytes 262144
  51.2 1.3 %copy.12 = f32[1,4096]{1,0:T(1,128)} copy(f32[1,4096]{1,0:T(1,128)} %get-tuple-element.5) | data formatting | bytes 32768

commit v7 on v6

--- a/solution.py
+++ b/solution.py
@@ -57,12 +57,19 @@
     return high, (value - high.astype(F32)).astype(BF16)
 
 
+def exchange(row, col, outer, inner):
+    shift_inner, shift_outer = inner.bit_length() - 1, outer.bit_length() - 1
+    same_outer = (row >> shift_inner) == (col & (outer - 1))
+    same_inner = (row & (inner - 1)) == (col >> shift_outer)
+    return jnp.logical_and(same_outer, same_inner).astype(F32).astype(BF16)
+
+
 def kernel(
     sizes, tile,
     inputs_hbm, cotangent_hbm, filters_hbm, forward_hbm, wave_hbm, twiddle_hbm, backward_hbm,
-    input_grad_ref, filter_grad_ref,
+    arrived, grad_in,
     inputs_ref, cotangent_ref, filters_ref, staged, staged_filter, gathered, spectrum, parts, result,
-    arrived, reduced_in, reduced_out, grad_in, forward_ref, wave_ref, twiddle_ref, backward_ref,
+    reduced_in, reduced_out, forward_ref, wave_ref, twiddle_ref, backward_ref,
     load_sem, table_sem, send_sem, data_sem, filter_send_sem, gather_send_sem, pass_send_sem, out_send_sem,
     reduce_send_sem, last_send_sem, part_sem, gather_sem, pass_sem, out_sem, reduce_sem, last_sem,
 ):
@@ -150,8 +157,7 @@
     count = zs * ROWS
     row = lax.broadcasted_iota(jnp.int32, (count, count), 0)
     col = lax.broadcasted_iota(jnp.int32, (count, count), 1)
-    regroup = jnp.logical_and(row // ROWS == col % zs, row % ROWS == col // zs).astype(F32).astype(BF16)
-    ungroup = jnp.logical_and(row % zs == col // ROWS, row // zs == col % ROWS).astype(F32).astype(BF16)
+    regroup = exchange(row, col, zs, ROWS)
 
     def stage(value):
         stacked = jnp.concatenate([value[:, a * inner:(a + 1) * inner] for a in range(ROWS)], axis=0)
@@ -348,21 +354,28 @@
         remote(*to_partner).wait_send()
 
     landed(arrived, out_sem)
+    landed(grad_in, last_sem)
+
+    @pl.when(core == 0)
+    def _():
+        left(result, blocks, xl == 0, out_send_sem)
+
+    @pl.when(core == 1)
+    def _():
+        landed(result.at[pl.ds(0, blocks - 2)], reduce_send_sem)
+        left(reduced_out, 2, own_last, last_send_sem)
+
+
+def unpack(arrived, grad_in, input_grad_ref, filter_grad_ref):
+    zs, _, inner = arrived.shape
+    count = zs * ROWS
+    row = lax.broadcasted_iota(jnp.int32, (count, count), 0)
+    col = lax.broadcasted_iota(jnp.int32, (count, count), 1)
+    ungroup = exchange(row, col, ROWS, zs)
     spread = dot(ungroup, arrived[...].reshape(count, inner)).astype(BF16)
     for a in range(ROWS):
         input_grad_ref[:, a * inner:(a + 1) * inner] = spread[a * zs:(a + 1) * zs]
-    landed(grad_in, last_sem)
-    for a in range(ROWS):
         filter_grad_ref[:, a * inner:(a + 1) * inner] = grad_in[a:a + 1]
-
-    @pl.when(core == 0)
-    def _():
-        left(result, blocks, xl == 0, out_send_sem)
-
-    @pl.when(core == 1)
-    def _():
-        landed(result.at[pl.ds(0, blocks - 2)], reduce_send_sem)
-        left(reduced_out, 2, own_last, last_send_sem)
 
 
 def shards(tables, inputs, cotangent, filters):
@@ -377,11 +390,11 @@
     vmem = pl.BlockSpec(memory_space=pltpu.VMEM)
     hbm = pl.BlockSpec(memory_space=pltpu.HBM)
     dma = pltpu.SemaphoreType.DMA
-    return pl.pallas_call(
+    arrived, grad_in = pl.pallas_call(
         functools.partial(kernel, (zs, groups, outer, inner), tile),
         out_shape=(
-            jax.ShapeDtypeStruct((rows, length), BF16),
-            jax.ShapeDtypeStruct((1, length), F32),
+            jax.ShapeDtypeStruct((zs, ROWS, inner), BF16),
+            jax.ShapeDtypeStruct((ROWS, inner), F32),
         ),
         in_specs=[hbm] * 7,
         out_specs=(vmem, vmem),
@@ -395,10 +408,8 @@
             pltpu.VMEM((2, outer, 2 * inner), F32),
             pltpu.VMEM((2, 2 * outer, inner), BF16),
             pltpu.VMEM((blocks, ROWS, inner), BF16),
-            pltpu.VMEM((zs, ROWS, inner), BF16),
             pltpu.VMEM((groups, 2, ROWS, inner), BF16),
             pltpu.VMEM((2, ROWS, inner), F32),
-            pltpu.VMEM((ROWS, inner), F32),
             *[pltpu.VMEM(table.shape, table.dtype) for table in tables],
             dma((3,)), dma((4,)), dma((2,)), dma((2,)), *[dma] * 12,
         ],
@@ -406,6 +417,15 @@
             collective_id=0, has_side_effects=True, vmem_limit_bytes=64 * 1024 * 1024
         ),
     )(inputs, cotangent, filters, *tables)
+    return pl.pallas_call(
+        unpack,
+        out_shape=(
+            jax.ShapeDtypeStruct((rows, length), BF16),
+            jax.ShapeDtypeStruct((1, length), F32),
+        ),
+        in_specs=[vmem] * 2,
+        out_specs=(vmem, vmem),
+    )(arrived, grad_in)
 
 
 def solution(mesh):

time: 53.4 us -> 52.2 us (0.978)
  local copies, waits for them, and re-layouts: 2.89 us -> 0 us
  Pallas kernels: 49 us -> 50.8 us
    unnamed x2 -> x0, local copies, waits for them, and re-layouts: 2.89 us -> none
    pallas_call x0 -> x1, Pallas kernels: none -> 1.76 us  [shards(): pl.pallas_call(unpack, out_shape=(jax.ShapeDtypeStruct((rows, length), BF...]
where the time goes in v7:
time: 52.2 us; the launch traced here: 51.4 us
  Pallas kernels  50.8 us (97%)
  between operations  0.64 us (1%)
    pallas_call x1, Pallas kernels, shards(): pl.pallas_call(functools.partial(kernel, (zs, groups, outer, inner), tile...  49 us
    pallas_call x1, Pallas kernels, shards(): pl.pallas_call(unpack, out_shape=(jax.ShapeDtypeStruct((rows, length), BF...  1.76 us

profile of v7, /device:TPU:6, one launch (start us, length us, event | category | flops | bytes accessed | tf_op | source)
XLA Modules:
  0.0 51.4 jit_solution(7700690390458125266)
XLA Ops:
  0.6 49.0 %shard_map.86 = (bf16[16,16,256]{2,1,0:T(8,128)(2,1)}, f32[16,256]{1,0:T(8,128)}) custom-call(bf16[16,4096]{1,0:T(8,128)(2,1)} %inputs_hbm.1, bf16[16,4096]{1,0:T(8,128)(2,1)} %cotangent_hbm.1, f32[16,4096]{1,0:T(8,128)} %filters_hbm.1, bf16[2,1024,512]{2,1,0:T(8,128)(2,1)} %constant.8.clone.forward_hbm, bf16[1024,512]{1,0:T(8,128)(2,1)} %constant.9.clone.wave_hbm, ...), custom_call_target="tpu_custom_call" | custom-call | tf_op jit(solution)/shard_map/pallas_call | solution.py:393
  49.7 1.8 %shard_map.87 = (bf16[16,4096]{1,0:T(8,128)(2,1)}, f32[1,4096]{1,0:T(1,128)}) custom-call(bf16[16,16,256]{2,1,0:T(8,128)(2,1)} %get-tuple-element.4.arrived, f32[16,256]{1,0:T(8,128)} %get-tuple-element.5.grad_in), custom_call_target="tpu_custom_call" | custom-call | tf_op jit(solution)/shard_map/pallas_call | solution.py:420

commit v8 on v7

--- a/solution.py
+++ b/solution.py
@@ -397,7 +397,7 @@
             jax.ShapeDtypeStruct((ROWS, inner), F32),
         ),
         in_specs=[hbm] * 7,
-        out_specs=(vmem, vmem),
+        out_specs=(hbm, hbm),
         scratch_shapes=[
             pltpu.VMEM((rows, length), BF16),
             pltpu.VMEM((rows, length), BF16),

time: 52.2 us -> 51.7 us (level)
  Pallas kernels: 50.8 us -> 50.2 us
    pallas_call x1, Pallas kernels: 49 us -> 48.5 us  [shards(): pl.pallas_call(functools.partial(kernel, (zs, groups, outer, inner), tile...]
where the time goes in v8:
time: 51.7 us; the launch traced here: 50.8 us
  Pallas kernels  50.2 us (97%)
  between operations  0.64 us (1%)
    pallas_call x1, Pallas kernels, shards(): pl.pallas_call(functools.partial(kernel, (zs, groups, outer, inner), tile...  48.5 us
    pallas_call x1, Pallas kernels, shards(): pl.pallas_call(unpack, out_shape=(jax.ShapeDtypeStruct((rows, length), BF...  1.76 us

profile of v8, /device:TPU:6, one launch (start us, length us, event | category | flops | bytes accessed | tf_op | source)
XLA Modules:
  0.0 50.8 jit_solution(10130871363739715792)
XLA Ops:
  0.6 48.5 %shard_map.86 = (bf16[16,16,256]{2,1,0:T(8,128)(2,1)}, f32[16,256]{1,0:T(8,128)}) custom-call(bf16[16,4096]{1,0:T(8,128)(2,1)} %inputs_hbm.1, bf16[16,4096]{1,0:T(8,128)(2,1)} %cotangent_hbm.1, f32[16,4096]{1,0:T(8,128)} %filters_hbm.1, bf16[2,1024,512]{2,1,0:T(8,128)(2,1)} %constant.8.clone.forward_hbm, bf16[1024,512]{1,0:T(8,128)(2,1)} %constant.9.clone.wave_hbm, ...), custom_call_target="tpu_custom_call" | custom-call | tf_op jit(solution)/shard_map/pallas_call | solution.py:393
  49.1 1.8 %shard_map.87 = (bf16[16,4096]{1,0:T(8,128)(2,1)}, f32[1,4096]{1,0:T(1,128)}) custom-call(bf16[16,16,256]{2,1,0:T(8,128)(2,1)} %get-tuple-element.4.arrived, f32[16,256]{1,0:T(8,128)} %get-tuple-element.5.grad_in), custom_call_target="tpu_custom_call" | custom-call | tf_op jit(solution)/shard_map/pallas_call | solution.py:420

commit v9 on v8

--- a/solution.py
+++ b/solution.py
@@ -12,6 +12,7 @@
 
 ROWS = 16
 BF16 = jnp.bfloat16
+FAR = (12, 10, 14, 5, 13, 8, 4, 3, 11, 7, 15, 1, 9, 2, 6, 0)
 NEAR = (8, 7, -7, 4, 6, 5, -4, 3, -3, 2, -1, 0, -6, -5, -2, 1)
 F32 = jnp.float32
 
@@ -195,6 +196,14 @@
         f = order(i)
         return staged_filter.at[f], late.at[ctx], filter_send_sem, part_sem, 2 * f + core, 2 * plane
 
+    def partner(k):
+        if groups != len(FAR):
+            return (place + 1 + k) & (groups - 1)
+        bits = 0
+        for n, value in enumerate(FAR):
+            bits = jnp.where(k == n, value, bits)
+        return place ^ bits
+
     def each(first, number, *many):
         def body(i, carry):
             for args in many:
@@ -210,7 +219,7 @@
     each(0, zs, rows(1, late))
 
     def gather_rows(k):
-        q = (place + 1 + k) & (groups - 1)
+        q = partner(k)
         block = late.at[pl.ds(2 * place, 2)]
         return block, block, gather_send_sem, gather_sem, 2 * z + (q & 1), q & -2
 
@@ -314,7 +323,7 @@
         return (z + off) & (zs - 1)
 
     def reduce_rows(k):
-        q = (place + 1 + k) & (groups - 1)
+        q = partner(k)
         return (
             result.at[pl.ds(2 * reduced_z(q), 2)], reduced_in.at[place], reduce_send_sem, reduce_sem,
             2 * z + (q & 1), (q & -2) + 1,

time: 51.7 us -> 51.5 us (level)
  no operation moved by 1% of the time
where the time goes in v9:
time: 51.5 us; the launch traced here: 51 us
  Pallas kernels  50.4 us (98%)
  between operations  0.64 us (1%)
    pallas_call x1, Pallas kernels, shards(): pl.pallas_call(functools.partial(kernel, (zs, groups, outer, inner), tile...  48.6 us
    pallas_call x1, Pallas kernels, shards(): pl.pallas_call(unpack, out_shape=(jax.ShapeDtypeStruct((rows, length), BF...  1.76 us

profile of v9, /device:TPU:6, one launch (start us, length us, event | category | flops | bytes accessed | tf_op | source)
XLA Modules:
  0.0 51.0 jit_solution(12367453723289880640)
XLA Ops:
  0.6 48.6 %shard_map.86 = (bf16[16,16,256]{2,1,0:T(8,128)(2,1)}, f32[16,256]{1,0:T(8,128)}) custom-call(bf16[16,4096]{1,0:T(8,128)(2,1)} %inputs_hbm.1, bf16[16,4096]{1,0:T(8,128)(2,1)} %cotangent_hbm.1, f32[16,4096]{1,0:T(8,128)} %filters_hbm.1, bf16[2,1024,512]{2,1,0:T(8,128)(2,1)} %constant.8.clone.forward_hbm, bf16[1024,512]{1,0:T(8,128)(2,1)} %constant.9.clone.wave_hbm, ...), custom_call_target="tpu_custom_call" | custom-call | tf_op jit(solution)/shard_map/pallas_call | solution.py:402
  49.2 1.8 %shard_map.87 = (bf16[16,4096]{1,0:T(8,128)(2,1)}, f32[1,4096]{1,0:T(1,128)}) custom-call(bf16[16,16,256]{2,1,0:T(8,128)(2,1)} %get-tuple-element.4.arrived, f32[16,256]{1,0:T(8,128)} %get-tuple-element.5.grad_in), custom_call_target="tpu_custom_call" | custom-call | tf_op jit(solution)/shard_map/pallas_call | solution.py:429
